TPU v7x, 32 devices: a whole 2x2x4 slice. The times are simulated.
32 devices in a mesh: shard: 8 (over y, x, core), tensor: 4 (over z).
Axes of the slice: x: 2, y: 2, z: 4, core: 2. Of those that a mesh axis runs over, the one named last changes fastest.
Arguments:
- hidden_in: bfloat16 [6144, 8192], P('shard'), may hold values from -720 to 720
- policy_weights: bfloat16 [2, 8192, 1024], P(None, 'shard', 'tensor'), may hold values from -6 to 6
- reference_weights: bfloat16 [2, 8192, 1024], P(None, None, 'tensor'), may hold values from -6 to 6
- policy_queries: bfloat16 [6144, 4096], P('shard', 'tensor'), may hold values from -180 to 180
- reference_queries: bfloat16 [6144, 4096], P('shard', 'tensor'), may hold values from -180 to 180
- readout: bfloat16 [6144, 4096], P('shard', 'tensor'), may hold values from -90 to 90
- lengths: int32 [16], P('shard'), may hold values from 96 to 384, as said below
Outputs:
- new_policy: bfloat16 [2, 8192, 1024], P(None, 'shard', 'tensor')
- new_reference: bfloat16 [2, 8192, 1024], P(None, None, 'tensor')
- margins: float32 [8], P('shard')
Inputs may be any that keep to these rules, and one draw needn't show every extreme that they name: The first lengths[s] positions of sequence s are real, the rest padding; some sequence has all 384 real.
All inputs are finite; a program needn't handle non-finite values.
Results may differ from a plain program's by a relative error of at most 0.0087.
Values may be sent and summed in bfloat16 or wider, within the bound.
No kernel may reach another device: no remote copies, remote signals or barrier semaphores. Data moves between devices by JAX's collectives and lax.ppermute only.
A program may use at most 128 MiB of HBM per device.

v0:
```python
import functools
import math

import jax
import jax.numpy as jnp
import numpy as np
from jax import lax
from jax.experimental import pallas as pl
from jax.experimental.pallas import tpu as pltpu
from jax.sharding import PartitionSpec as P

D = 8192
HD = 128
KVH = 8
QH = 32
LEN = 384
TILE = 128

rope_base = 1000000.0
dpo_beta = 0.1
learning_rate = 0.2
mix_alpha = 0.6
norm_eps = 1e-06
width_scale = D ** (-0.5)
logit_scale = 1.0 / math.sqrt(HD)
MIB = 1024 * 1024

NT = (((1,), (1,)), ((), ()))
NN = (((1,), (0,)), ((), ()))
TN = (((0,), (0,)), ((), ()))


def dot(a, b, dims):
    return lax.dot_general(a, b, dims, preferred_element_type=jnp.float32)


def params(mib=48):
    return pltpu.CompilerParams(vmem_limit_bytes=mib * MIB)


VMEM = pl.BlockSpec(memory_space=pltpu.VMEM)
SMEM = pl.BlockSpec(memory_space=pltpu.SMEM)
HBM = pl.BlockSpec(memory_space=pl.ANY)


def resident(x):
    return pltpu.with_memory_space_constraint(x, pltpu.VMEM)


def rope_tables():
    frequency = rope_base ** (-2.0 * np.arange(HD // 2) / HD)
    angles = np.arange(LEN)[:, None] * frequency[None, :]
    cosine, sine = np.cos(angles), np.sin(angles)
    return (
        np.concatenate([cosine, cosine], axis=1).astype(np.float32),
        np.concatenate([-sine, sine], axis=1).astype(np.float32),
    )


def store_heads(acc_ref, cos, sin, key_ref, value_ref):
    for s in range(key_ref.shape[0] // LEN):
        rows = slice(s * LEN, (s + 1) * LEN)
        for h in range(key_ref.shape[1] // HD):
            cols = slice(h * HD, (h + 1) * HD)
            k = acc_ref[0, rows, cols] * width_scale
            key_ref[rows, cols] = (k * cos + pltpu.roll(k, HD // 2, 1) * sin).astype(jnp.bfloat16)
    value_ref[...] = (acc_ref[1] * width_scale).astype(jnp.bfloat16)


def norm_project_kernel(hidden_hbm, weight_hbm, cos_ref, sin_ref, normed_ref, key_ref, value_ref, x, w, acc, part, in_sem, w_sem):
    tokens = x.shape[0]
    step, width, span, chunk = 16, 512, 128, 1024
    reads = []
    for i in range(tokens // span):
        at = pl.ds(i * span, span)
        reads.append(pltpu.make_async_copy(hidden_hbm.at[at], x.at[at], in_sem.at[i]))
    loads = []
    for c in range(D // chunk):
        at = pl.ds(c * chunk, chunk)
        loads.append(pltpu.make_async_copy(weight_hbm.at[:, at, :], w.at[:, at, :], w_sem.at[c]))
    for copy in reads + loads:
        copy.start()

    def row_step(i, carry):
        at = pl.ds(pl.multiple_of(i * step, step), step)
        total = jnp.zeros((step, width), jnp.float32)
        for c in range(D // width):
            v = x[at, c * width : (c + 1) * width].astype(jnp.float32)
            total = total + v * v
        part[at, :] = functools.reduce(jnp.add, [total[:, c * 128 : (c + 1) * 128] for c in range(width // 128)])
        return carry

    for i, copy in enumerate(reads):
        copy.wait()
        lax.fori_loop(i * (span // step), (i + 1) * (span // step), row_step, 0)
    for copy in loads:
        copy.wait()
    mean = jnp.sum(part[...], axis=1, keepdims=True) * (1.0 / D)
    part[...] = jnp.broadcast_to(lax.rsqrt(mean + norm_eps), part.shape)

    def normalise(c):
        at = slice(c * chunk, (c + 1) * chunk)
        for i in range(tokens // span):
            rows = slice(i * span, (i + 1) * span)
            scale = jnp.concatenate([part[rows, :]] * (chunk // 128), axis=1)
            normed_ref[rows, at] = (x[rows, at].astype(jnp.float32) * scale).astype(jnp.bfloat16)

    normalise(0)
    for c in range(D // chunk):
        at = slice(c * chunk, (c + 1) * chunk)
        for i in (0, 1):
            term = dot(normed_ref[:, at], w[i, at, :], NN)
            acc[i] = term if c == 0 else acc[i] + term
        if (c + 1) * chunk < D:
            normalise(c + 1)
    store_heads(acc, cos_ref[...], sin_ref[...], key_ref, value_ref)


def norm_project(hidden, weights, cos, sin):
    tokens = hidden.shape[0]
    cols = weights.shape[2]
    return pl.pallas_call(
        norm_project_kernel,
        in_specs=[HBM, HBM, VMEM, VMEM],
        out_specs=[VMEM, VMEM, VMEM],
        out_shape=[
            pltpu.VMEM((tokens, D), jnp.bfloat16),
            jax.ShapeDtypeStruct((tokens, cols), jnp.bfloat16),
            jax.ShapeDtypeStruct((tokens, cols), jnp.bfloat16),
        ],
        scratch_shapes=[
            pltpu.VMEM((tokens, D), jnp.bfloat16),
            pltpu.VMEM((2, D, cols), jnp.bfloat16),
            pltpu.VMEM((2, tokens, cols), jnp.float32),
            pltpu.VMEM((tokens, 128), jnp.float32),
            pltpu.SemaphoreType.DMA((tokens // 128,)),
            pltpu.SemaphoreType.DMA((D // 1024,)),
        ],
        compiler_params=params(),
        cost_estimate=pl.CostEstimate(flops=4 * tokens * D * cols, bytes_accessed=4 * tokens * D + 4 * D * cols, transcendentals=0),
        name="norm_project",
    )(hidden, weights, cos, sin)


def project_kernel(count, first, last, idx_ref, masks_ref, x_ref, *refs):
    refs = list(refs)
    pieces = [refs[:count], refs[count : 2 * count]]
    refs = refs[2 * count :]
    held = None if first else refs.pop(0)
    if last:
        cos_ref, sin_ref, key_ref, value_ref, w, acc, sem = refs
    else:
        acc, w, sem = refs
    depth = w.shape[2]
    copies = [[pltpu.make_async_copy(pieces[i][n], w.at[i, n], sem.at[i, n]) for i in (0, 1)] for n in range(count)]
    for pair in copies:
        for copy in pair:
            copy.start()
    for n in range(count):
        for copy in copies[n]:
            copy.wait()
        col = pl.multiple_of((idx_ref[0] ^ masks_ref[n]) * depth, depth)
        x = x_ref[:, pl.ds(col, depth)]
        for i in (0, 1):
            term = dot(x, w[i, n], NN)
            if n:
                term = acc[i] + term
            elif not first:
                term = held[i] + term
            acc[i] = term
    if last:
        store_heads(acc, cos_ref[...], sin_ref[...], key_ref, value_ref)


def project(idx, normed, masks, pieces, held, tables):
    tokens = normed.shape[0]
    rows, cols = pieces[masks[0]][0].shape
    first, last = held is None, tables is not None
    count = len(masks)
    in_specs = [SMEM, SMEM, VMEM] + [HBM] * (2 * count)
    args = [idx, jnp.asarray(masks, jnp.int32), resident(normed)]
    args += [pieces[m][0] for m in masks] + [pieces[m][1] for m in masks]
    if not first:
        in_specs.append(VMEM)
        args.append(held)
    acc_shape = (2, tokens, cols)
    scratch = [pltpu.VMEM((2, count, rows, cols), jnp.bfloat16), pltpu.SemaphoreType.DMA((2, count))]
    if last:
        in_specs += [VMEM] * 2
        args += list(tables)
        out_specs = [VMEM] * 2
        out_shape = [jax.ShapeDtypeStruct((tokens, cols), jnp.bfloat16)] * 2
        scratch.insert(1, pltpu.VMEM(acc_shape, jnp.float32))
    else:
        out_specs = VMEM
        out_shape = jax.ShapeDtypeStruct(acc_shape, jnp.float32)
    return pl.pallas_call(
        functools.partial(project_kernel, count, first, last),
        in_specs=in_specs,
        out_specs=out_specs,
        out_shape=out_shape,
        scratch_shapes=scratch,
        compiler_params=params(),
        cost_estimate=pl.CostEstimate(
            flops=4 * tokens * rows * cols * count,
            bytes_accessed=count * (2 * tokens * rows + 4 * rows * cols),
            transcendentals=0,
        ),
        name="project",
    )(*args)


def stacked(ref, r, groups):
    rows = slice(r * TILE, (r + 1) * TILE)
    return jnp.concatenate([ref[rows, g * HD : (g + 1) * HD] for g in range(groups)], axis=0)


def live_readout(ref, r, groups, length):
    x = stacked(ref, r, groups).astype(jnp.float32)
    at = lax.broadcasted_iota(jnp.int32, x.shape, 0) % TILE + r * TILE
    return jnp.where(at < length, x, 0.0).astype(jnp.bfloat16)


def attend_kernel(back, len_ref, q_ref, k_ref, v_ref, ro_ref, *rest):
    groups = q_ref.shape[1] // HD
    seq = pl.program_id(0)
    length = len_ref[seq]
    tiles = LEN // TILE
    if back:
        before_ref, cos_ref, sin_ref, margin_ref, grad_ref = rest
    else:
        (margin_ref,) = rest
    side = jnp.where(seq % 2 == 0, 1.0, -1.0) * (dpo_beta / math.sqrt(QH * HD))
    score = jnp.zeros((1, groups * TILE), jnp.float32)
    dk = [None] * tiles
    dv = [None] * tiles
    for r in range(tiles):
        n = (r + 1) * TILE
        q = stacked(q_ref, r, groups)
        ro = live_readout(ro_ref, r, groups, length)
        s = dot(k_ref[0:n, :], q, NT)
        dp = dot(v_ref[0:n, :], ro, NT)
        j = lax.broadcasted_iota(jnp.int32, (TILE, groups * TILE), 0)
        i = lax.broadcasted_iota(jnp.int32, (TILE, groups * TILE), 1) % TILE
        s = [s[b * TILE : (b + 1) * TILE] for b in range(r + 1)]
        s[r] = jnp.where(j <= i, s[r], -1e30)
        top = functools.reduce(jnp.maximum, [jnp.max(x, axis=0, keepdims=True) for x in s])
        e = [jnp.exp2((x - top) * (logit_scale * math.log2(math.e))) for x in s]
        inverse = 1.0 / functools.reduce(jnp.add, [jnp.sum(x, axis=0, keepdims=True) for x in e])
        dp = [dp[b * TILE : (b + 1) * TILE] for b in range(r + 1)]
        p = [(x * inverse).astype(jnp.bfloat16) for x in e]
        wide = [x.astype(jnp.float32) for x in p]
        delta = functools.reduce(jnp.add, [jnp.sum(x * y, axis=0, keepdims=True) for x, y in zip(wide, dp)])
        score = score + delta
        if back:
            ds = jnp.concatenate([(x * (y - delta)).astype(jnp.bfloat16) for x, y in zip(wide, dp)], axis=0)
            tk = dot(ds, q, NN)
            tv = dot(jnp.concatenate(p, axis=0), ro, NN)
            for b in range(r + 1):
                at = slice(b * TILE, (b + 1) * TILE)
                dk[b] = tk[at] if dk[b] is None else dk[b] + tk[at]
                dv[b] = tv[at] if dv[b] is None else dv[b] + tv[at]
    @pl.when((seq == 0) & (pl.program_id(1) == 0))
    def _():
        margin_ref[...] = -before_ref[...] if back else jnp.zeros_like(margin_ref)

    margin_ref[...] += jnp.broadcast_to(jnp.sum(score, axis=1, keepdims=True) * side, margin_ref.shape)
    if back:
        scale = jnp.where(seq % 2 == 0, -1.0, 1.0) * (1.0 / math.sqrt(QH * HD))
        for b in range(tiles):
            at = slice(b * TILE, (b + 1) * TILE)
            k = dk[b] * (scale * logit_scale)
            grad_ref[0, at, :] = (k * cos_ref[at, :] - pltpu.roll(k, HD // 2, 1) * sin_ref[at, :]).astype(jnp.bfloat16)
            grad_ref[1, at, :] = (dv[b] * scale).astype(jnp.bfloat16)


def attend(lengths, queries, keys, values, readout, before=None, tables=None):
    seqs = lengths.shape[0]
    heads = keys.shape[1] // HD
    wide = queries.shape[1] // heads
    back = tables is not None
    at = lambda s, k, lens: (s, k)
    in_specs = [
        pl.BlockSpec((LEN, wide), at),
        pl.BlockSpec((LEN, HD), at),
        pl.BlockSpec((LEN, HD), at),
        pl.BlockSpec((LEN, wide), at),
    ]
    args = [queries, keys, values, readout]
    fixed = lambda s, k, lens: (0, 0)
    out_specs = [pl.BlockSpec((8, 128), fixed)]
    out_shape = [jax.ShapeDtypeStruct((8, 128), jnp.float32)]
    if back:
        in_specs += [pl.BlockSpec((8, 128), fixed)] + [pl.BlockSpec((LEN, HD), fixed)] * 2
        args += [before, *tables]
        out_specs.append(pl.BlockSpec((2, LEN, HD), lambda s, k, lens: (0, s, k)))
        out_shape.append(jax.ShapeDtypeStruct((2,) + keys.shape, jnp.bfloat16))
    return pl.pallas_call(
        functools.partial(attend_kernel, back),
        grid_spec=pltpu.PrefetchScalarGridSpec(num_scalar_prefetch=1, grid=(seqs, heads), in_specs=in_specs, out_specs=out_specs),
        out_shape=out_shape,
        compiler_params=params(),
        cost_estimate=pl.CostEstimate(
            flops=seqs * heads * LEN * LEN * wide * (8 if back else 4),
            bytes_accessed=4 * seqs * LEN * wide * heads,
            transcendentals=seqs * heads * LEN * LEN * wide // HD,
        ),
        name="attend_back" if back else "attend",
    )(lengths, *args)


def gradient_tiles(idx, mask, x_ref, cot_ref, rows):
    both = jnp.concatenate([cot_ref[0], cot_ref[1]], axis=1)
    tile = min(rows, 512)
    for t in range(rows // tile):
        col = pl.multiple_of((idx ^ mask) * rows + t * tile, tile)
        out = dot(x_ref[:, pl.ds(col, tile)], both, TN)
        for i in (0, 1):
            yield i, slice(t * tile, (t + 1) * tile), out[:, i * cot_ref.shape[2] : (i + 1) * cot_ref.shape[2]]


def gradient_kernel(mask, idx_ref, x_ref, cot_ref, out_ref):
    for i, at, value in gradient_tiles(idx_ref[0], mask, x_ref, cot_ref, out_ref.shape[1]):
        out_ref[i, at, :] = value.astype(out_ref.dtype)


def merged_kernel(mask, idx_ref, x_ref, cot_ref, theirs_ref, mine_margin, their_margin, *outs):
    cols = cot_ref.shape[2]
    wide = lambda ref: jnp.concatenate([jax.nn.sigmoid(-ref[0:1, :])] * (cols // 128), axis=1)
    mine, their = wide(mine_margin), wide(their_margin)
    for i, at, value in gradient_tiles(idx_ref[0], mask, x_ref, cot_ref, theirs_ref.shape[1]):
        value = value * mine + theirs_ref[i, at, :].astype(jnp.float32) * their
        outs[i][at, :] = value.astype(outs[i].dtype)


def gradient_block(idx, normed, cot, mask, rows, merge=None):
    _, tokens, cols = cot.shape
    args = [idx, resident(normed), cot]
    if merge is None:
        kernel, name = gradient_kernel, "gradient_block"
        out_shape = jax.ShapeDtypeStruct((2, rows, cols), jnp.bfloat16)
    else:
        kernel, name = merged_kernel, "merged_block"
        args += list(merge)
        out_shape = [jax.ShapeDtypeStruct((rows, cols), jnp.bfloat16 if mask else jnp.float32)] * 2
    return pl.pallas_call(
        functools.partial(kernel, mask),
        in_specs=[SMEM] + [VMEM] * (len(args) - 1),
        out_specs=VMEM if merge is None else [VMEM] * 2,
        out_shape=out_shape,
        compiler_params=params(),
        cost_estimate=pl.CostEstimate(flops=4 * tokens * rows * cols, bytes_accessed=8 * rows * cols, transcendentals=0),
        name=name,
    )(*args)


def finish_kernel(counts, *refs):
    refs = list(refs)
    *outs, square_ref = refs[-3:]
    refs = refs[:-3]
    square_ref[...] = jnp.zeros_like(square_ref)
    for i in (0, 1):
        value = refs.pop(0)[...]
        for _ in range(counts[i]):
            value = value + refs.pop(0)[...].astype(jnp.float32)
        outs[i][...] = value.astype(jnp.bfloat16)
        total = jnp.sum(jnp.sum(value * value, axis=0, keepdims=True), axis=1, keepdims=True)
        square_ref[i : i + 1, :] = jnp.broadcast_to(total, (1, 128))


def finish(base, arrived):
    args = [x for i in (0, 1) for x in (base[i], *arrived[i])]
    return pl.pallas_call(
        functools.partial(finish_kernel, [len(a) for a in arrived]),
        in_specs=[VMEM] * len(args),
        out_specs=[VMEM] * 3,
        out_shape=[jax.ShapeDtypeStruct(base[0].shape, jnp.bfloat16)] * 2 + [jax.ShapeDtypeStruct((8, 128), jnp.float32)],
        compiler_params=params(),
        name="finish",
    )(*args)


def blend_kernel(count, first, idx_ref, masks_ref, square_ref, *refs):
    refs = list(refs)
    pieces = [[refs[(2 * k + i) * count : (2 * k + i + 1) * count] for i in (0, 1)] for k in (0, 1)]
    refs = refs[4 * count :]
    ref_hbm = refs.pop(0)
    if not first:
        refs.pop(0)
    out_hbm, token_ref = refs[:2]
    new_hbm = refs[2] if first else None
    x, r, o, new, sem, out_sem = refs[3 if first else 2 :]
    rows, cols = r.shape[2:]
    token_ref[...] = jnp.zeros_like(token_ref)
    copies, at = [], []
    for n in range(count):
        at.append(pl.ds(pl.multiple_of((idx_ref[0] ^ masks_ref[n]) * rows, rows), rows))
        group = [pltpu.make_async_copy(pieces[k][i][n], x.at[k, i, n], sem.at[2 * k + i, n]) for k in (0, 1) for i in (0, 1)]
        group.append(pltpu.make_async_copy(ref_hbm.at[:, at[n], :], r.at[n], sem.at[4, n]))
        for copy in group:
            copy.start()
        copies.append(group)
    mean = square_ref[...] * (1.0 / (D * KVH * HD))
    scale = jnp.concatenate([learning_rate * lax.rsqrt(mean + norm_eps)] * (cols // 128), axis=1)
    writes = []
    for n in range(count):
        for copy in copies[n]:
            copy.wait()
        for i in (0, 1):
            value = (x[0, i, n].astype(jnp.float32) - scale[i : i + 1, :] * x[1, i, n].astype(jnp.float32)).astype(jnp.bfloat16)
            if first and n == 0:
                new[i] = value
            mixed = mix_alpha * value.astype(jnp.float32) + (1.0 - mix_alpha) * r[n, i].astype(jnp.float32)
            o[n, i] = mixed.astype(jnp.bfloat16)
        writes.append(pltpu.make_async_copy(o.at[n], out_hbm.at[:, at[n], :], out_sem.at[n]))
        if first and n == 0:
            writes.append(pltpu.make_async_copy(new, new_hbm, out_sem.at[count]))
            writes[-1].start()
        writes[len(writes) - 1 - (first and n == 0)].start()
    for copy in writes:
        copy.wait()


def blend(idx, squares, weights, grads, reference, held, masks):
    rows, cols = weights[masks[0]][0].shape
    count = len(masks)
    first = held is None
    args = [idx, jnp.asarray(masks, jnp.int32), squares]
    args += [pieces[m][i] for pieces in (weights, grads) for i in (0, 1) for m in masks] + [reference]
    in_specs = [SMEM, SMEM, VMEM] + [HBM] * (4 * count + 1)
    out_specs = [HBM, VMEM]
    out_shape = [jax.ShapeDtypeStruct(reference.shape, jnp.bfloat16), jax.ShapeDtypeStruct((8, 128), jnp.float32)]
    aliases = {}
    if first:
        out_specs.append(HBM)
        out_shape.append(jax.ShapeDtypeStruct((2, rows, cols), jnp.bfloat16))
    else:
        aliases = {len(args): 0}
        in_specs.append(HBM)
        args.append(held)
    return pl.pallas_call(
        functools.partial(blend_kernel, count, first),
        in_specs=in_specs,
        out_specs=out_specs,
        out_shape=out_shape,
        scratch_shapes=[
            pltpu.VMEM((2, 2, count, rows, cols), jnp.bfloat16),
            pltpu.VMEM((count, 2, rows, cols), jnp.bfloat16),
            pltpu.VMEM((count, 2, rows, cols), jnp.bfloat16),
            pltpu.VMEM((2, rows, cols), jnp.bfloat16),
            pltpu.SemaphoreType.DMA((5, count)),
            pltpu.SemaphoreType.DMA((count + 1,)),
        ],
        input_output_aliases=aliases,
        compiler_params=params(62),
        cost_estimate=pl.CostEstimate(flops=8 * rows * cols * count, bytes_accessed=16 * rows * cols * count, transcendentals=0),
        name="blend",
    )(*args)


def bits_of(mask):
    return [1 << b for b in range(mask.bit_length()) if mask >> b & 1]


def after(value, *earlier):
    return lax.optimization_barrier((value, earlier))[0]


def body(shards, tensors, hidden_in, policy_weights, reference_weights, policy_queries, reference_queries, readout, lengths):
    rows = policy_weights.shape[1]
    idx = lax.axis_index("shard").astype(jnp.int32).reshape(1)
    tables = tuple(jnp.asarray(t) for t in rope_tables())

    def swap(x, bit, axis="shard", size=shards):
        return lax.ppermute(x, axis, [(i, i ^ bit) for i in range(size)])

    def powers(size):
        return [1 << b for b in range(size.bit_length() - 1)]

    chips = sorted(range(0, shards, 2), key=lambda m: (len(bits_of(m)), m))
    near = [m for m in chips if len(bits_of(m)) == 1]
    far = [m for m in chips if len(bits_of(m)) > 1]
    link = lambda i, m: bits_of(m)[-1] if i == 0 else bits_of(m)[0]

    def send_near(own):
        got = {0: list(own)}
        for turn in (0, 1):
            for n, m in enumerate(near):
                i = (turn + n) % 2
                got.setdefault(m, [None, None])[i] = swap(own[i], m)
        got[1] = [swap(g, 1) for g in own]
        return got

    def relay(got, m, *earlier):
        got[m] = [None, None]
        for i in (0, 1):
            via = link(i, m)
            got[m][i] = swap(after(got[m ^ via][i], *earlier), via)

    def to_core(got, m, *earlier):
        got[m | 1] = [swap(after(g, *earlier), 1) for g in got[m]]

    weights = send_near((policy_weights[0], policy_weights[1]))
    normed, ref_keys, ref_values = norm_project(hidden_in, reference_weights, *tables)
    for m in far:
        relay(weights, m, ref_keys)
    for m in near:
        to_core(weights, m, ref_keys)
    (ref_margin,) = attend(lengths, reference_queries, ref_keys, ref_values, readout)
    early = [m | c for m in [0] + near for c in (0, 1)]
    held = project(after(idx, ref_margin), normed, early, weights, None, None if far else tables)
    if far:
        for m in far:
            to_core(weights, m, held)
        held = project(idx, normed, [m | c for m in far for c in (0, 1)], weights, held, tables)
    pol_keys, pol_values = held
    margin, cot = attend(lengths, policy_queries, pol_keys, pol_values, readout, ref_margin, tables)

    theirs = {}
    order = list(reversed(chips))

    def block_for_core(earlier):
        m = order[len(theirs)]
        block = gradient_block(after(idx, earlier), normed, cot, m | 1, rows)
        theirs[m] = swap(block, 1)
        return block

    for bit in powers(tensors):
        received = swap(margin, bit, "tensor", tensors)
        if len(theirs) < len(order) - 1:
            received = after(received, block_for_core(margin))
        margin = margin + received
    other = swap(margin, 1)
    if len(theirs) < len(order) - 1:
        other = after(other, block_for_core(margin))

    chip_sum = {}
    arrived = {m: [[], []] for m in chips}
    waiting = []
    last = other

    def send(m, i):
        payload = chip_sum[m][i]
        if arrived[m][i]:
            payload = payload.astype(jnp.float32)
            for term in arrived[m][i]:
                payload = payload + term.astype(jnp.float32)
            payload = payload.astype(jnp.bfloat16)
        via = link(i, m)
        arrived[m ^ via][i].append(swap(payload, via))
        return payload

    for m in order:
        if m == 0:
            last = [send(*which) for which in waiting]
        if m not in theirs:
            last = block_for_core(last)
        chip_sum[m] = gradient_block(after(idx, last), normed, cot, m, rows, (theirs[m], margin, other))
        last = []
        for i in (0, 1):
            if m and not any(k ^ link(i, k) == m for k in far):
                last.append(send(m, i))
            elif m:
                waiting.append((m, i))
        last = last or chip_sum[m]
    *own, squares = finish(chip_sum[0], arrived[0])

    grads = send_near(own)
    for bit in powers(tensors):
        squares = squares + swap(squares, bit, "tensor", tensors)
    for m in far:
        relay(grads, m, squares)
        squares = after(squares, *[grads[m ^ link(i, m)][i] for i in (0, 1)])
    for bit in powers(shards):
        squares = squares + swap(squares, bit)
    for m in near:
        to_core(grads, m, squares)
    new_reference, token, new_policy = blend(idx, squares, weights, grads, reference_weights, None, [0, 1])
    new_reference, token = blend(idx, squares, weights, grads, reference_weights, new_reference, early[2:])
    for m in far:
        to_core(grads, m, token)
    for masks in (far, [m | 1 for m in far]) if far else ():
        new_reference, token = blend(idx, squares, weights, grads, reference_weights, new_reference, masks)
    return (new_policy, new_reference, margin[0, :1])


def solution(mesh):
    return jax.shard_map(
        functools.partial(body, mesh.shape["shard"], mesh.shape["tensor"]),
        mesh=mesh,
        in_specs=(
            P("shard", None),
            P(None, "shard", "tensor"),
            P(None, None, "tensor"),
            P("shard", "tensor"),
            P("shard", "tensor"),
            P("shard", "tensor"),
            P("shard"),
        ),
        out_specs=(P(None, "shard", "tensor"), P(None, None, "tensor"), P("shard")),
        check_vma=False,
    )
```

profile of v0, /device:TPU:0, one launch (start us, length us, event | category | flops | bytes accessed | tf_op | source)
XLA Modules:
  0.0 216.4 jit_solution(16309126972797221494)
XLA Ops:
  0.6 2.1 slice_bitcast_fusion
  2.7 2.9 %collective-permute-start = (bf16[1024,256]{1,0:T(8,128)(2,1)S(1)}, bf16[1024,256]{1,0:T(8,128)(2,1)}, u32[]{:S(2)}, u32[]{:S(2)}) collective-permute-start(bf16[1024,256]{1,0:T(8,128)(2,1)S(1)} %get-tuple-element.106.refs_0_), channel_id=1, source_target_pairs={{0,8},{4,12},{8,0},{12,4},{16,24},{20,28},{24,16},{28,20},{1,9},{5... | collective-permute-start | bytes 1572872 | tf_op jit(solution)/shard_map/ppermute | solution.py:475
  5.7 1.5 collective-permute-start.4
  7.8 16.4 %norm_project.1 = (bf16[768,8192]{1,0:T(8,128)(2,1)S(1)}, bf16[768,256]{1,0:T(8,128)(2,1)}, bf16[768,256]{1,0:T(8,128)(2,1)}) custom-call(bf16[768,8192]{1,0:T(8,128)(2,1)} %hidden_hbm.1, bf16[2,8192,256]{2,1,0:T(8,128)(2,1)} %refs_4_.3, f32[384,128]{1,0:T(8,128)} %constant.22.clone.cos_ref.refs_5_.rest_1_, f32[384,128]{1,0:T(8,128)} %constant.23.clone.sin_ref.refs_6_.rest_2_), custom_call_target="tpu_custom_call" | custom-call | flops 6442450944 | bytes 33554432 | tf_op jit(solution)/shard_map/norm_project/pallas_call | solution.py:122
  24.2 4.6 %copy-done = bf16[768,8192]{1,0:T(8,128)(2,1)} copy-done((bf16[768,8192]{1,0:T(8,128)(2,1)}, bf16[768,8192]{1,0:T(8,128)(2,1)S(1)}, u32[]{:S(2)}) %copy-start) | copy-done | bytes 12582936
  29.4 1.9 collective-permute-done.9.refs_10_.refs_6_
  31.8 1.5 collective-permute-start.1
  34.2 1.0 copy-done.16
  35.2 1.0 copy-done.17
  36.2 4.9 %attend.1.rest_0_ = f32[8,128]{1,0:T(8,128)S(1)} custom-call(s32[2]{0:T(128)S(1)} %copy-done.15, bf16[768,1024]{1,0:T(8,128)(2,1)S(1)} %copy-done.10, bf16[768,256]{1,0:T(8,128)(2,1)S(1)} %copy-done.16, bf16[768,256]{1,0:T(8,128)(2,1)S(1)} %copy-done.17, bf16[768,1024]{1,0:T(8,128)(2,1)S(1)} %copy-done.12), custom_call_target="tpu_custom_call" | custom-call | flops 1207959552 | bytes 3145728 | tf_op jit(solution)/shard_map/attend/pallas_call | solution.py:298
  41.6 4.6 %copy-done.1 = bf16[768,8192]{1,0:T(8,128)(2,1)S(1)} copy-done((bf16[768,8192]{1,0:T(8,128)(2,1)S(1)}, bf16[768,8192]{1,0:T(8,128)(2,1)}, u32[]{:S(2)}) %copy-start.1) | copy-done | bytes 12582936
  46.2 8.4 %project.2.refs_4_ = f32[2,768,256]{2,1,0:T(8,128)} custom-call(s32[1]{0:T(128)} %bitcast.idx_ref, s32[6]{0:T(128)} %call_exported.0.masks_ref, bf16[768,8192]{1,0:T(8,128)(2,1)S(1)} %copy-done.1, bf16[1024,256]{1,0:T(8,128)(2,1)} %copy-done.18, bf16[1024,256]{1,0:T(8,128)(2,1)} %collective-permute-done.2.refs_1_, ...), custom_call_target="tpu_custom_call" | custom-call | flops 4831838208 | bytes 15728640 | tf_op jit(solution)/shard_map/project/pallas_call | solution.py:197
  55.2 1.7 collective-permute-done.11.refs_1_.refs_0_
  57.7 5.6 %project.3 = (bf16[768,256]{1,0:T(8,128)(2,1)}, bf16[768,256]{1,0:T(8,128)(2,1)}) custom-call(s32[1]{0:T(128)} %bitcast.idx_ref, s32[2]{0:T(128)} %constant.24.clone.masks_ref, bf16[768,8192]{1,0:T(8,128)(2,1)S(1)} %copy-done.1, bf16[1024,256]{1,0:T(8,128)(2,1)} %collective-permute-done.1.refs_0_, bf16[1024,256]{1,0:T(8,128)(2,1)} %collective-permute-done.11.refs_1_.refs_0_, ...), custom_call_target="tpu_custom_call" | custom-call | flops 1610612736 | bytes 5242880 | tf_op jit(solution)/shard_map/project/pallas_call | solution.py:197
  63.4 1.0 copy-done.13
  64.4 1.0 copy-done.14
  65.4 8.7 %attend_back.1 = (f32[8,128]{1,0:T(8,128)S(1)}, bf16[2,768,256]{2,1,0:T(8,128)(2,1)S(1)}) custom-call(s32[2]{0:T(128)S(1)} %copy-done.15, bf16[768,1024]{1,0:T(8,128)(2,1)S(1)} %copy-done.11, bf16[768,256]{1,0:T(8,128)(2,1)S(1)} %copy-done.13, bf16[768,256]{1,0:T(8,128)(2,1)S(1)} %copy-done.14, bf16[768,1024]{1,0:T(8,128)(2,1)S(1)} %copy-done.12, ...), custom_call_target="tpu_custom_call" | custom-call | flops 2415919104 | bytes 3145728 | tf_op jit(solution)/shard_map/attend_back/pallas_call | solution.py:298
  75.0 4.6 %copy-done.2 = bf16[768,8192]{1,0:T(8,128)(2,1)S(1)} copy-done((bf16[768,8192]{1,0:T(8,128)(2,1)S(1)}, bf16[768,8192]{1,0:T(8,128)(2,1)}, u32[]{:S(2)}) %copy-start.2) | copy-done | bytes 12582936
  79.5 3.1 %gradient_block.4 = bf16[2,1024,256]{2,1,0:T(8,128)(2,1)} custom-call(s32[1]{0:T(128)} %bitcast.idx_ref, bf16[768,8192]{1,0:T(8,128)(2,1)S(1)} %copy-done.2, bf16[2,768,256]{2,1,0:T(8,128)(2,1)} %copy-done.3), custom_call_target="tpu_custom_call" | custom-call | flops 805306368 | bytes 2097152 | tf_op jit(solution)/shard_map/gradient_block/pallas_call | solution.py:346
  82.8 1.6 collective-permute-start.14
  84.4 2.0 collective-permute-done.14
  86.4 2.6 %collective-permute-start.15 = (f32[8,128]{1,0:T(8,128)S(1)}, f32[8,128]{1,0:T(8,128)S(1)}, u32[]{:S(2)}, u32[]{:S(2)}) collective-permute-start(f32[8,128]{1,0:T(8,128)S(1)} %add.27), channel_id=1, source_target_pairs={{0,2},{1,3},{2,0},{3,1},{4,6},{5,7},{6,4},{7,5},{8,10},{9,11},{10,... | collective-permute-start | bytes 12296 | tf_op jit(solution)/shard_map/ppermute | solution.py:475
  89.0 3.1 %gradient_block.5 = bf16[2,1024,256]{2,1,0:T(8,128)(2,1)} custom-call(s32[1]{0:T(128)} %bitcast.idx_ref, bf16[768,8192]{1,0:T(8,128)(2,1)S(1)} %copy-done.2, bf16[2,768,256]{2,1,0:T(8,128)(2,1)} %copy-done.3), custom_call_target="tpu_custom_call" | custom-call | flops 805306368 | bytes 2097152 | tf_op jit(solution)/shard_map/gradient_block/pallas_call | solution.py:346
  92.2 3.1 %gradient_block.6 = bf16[2,1024,256]{2,1,0:T(8,128)(2,1)} custom-call(s32[1]{0:T(128)} %bitcast.idx_ref, bf16[768,8192]{1,0:T(8,128)(2,1)S(1)} %copy-done.2, bf16[2,768,256]{2,1,0:T(8,128)(2,1)} %copy-done.3), custom_call_target="tpu_custom_call" | custom-call | flops 805306368 | bytes 2097152 | tf_op jit(solution)/shard_map/gradient_block/pallas_call | solution.py:346
  95.8 2.2 collective-permute-done.16.their_margin
  98.6 1.0 copy-done.19
  99.5 3.5 %merged_block.4 = (bf16[1024,256]{1,0:T(8,128)(2,1)}, bf16[1024,256]{1,0:T(8,128)(2,1)}) custom-call(s32[1]{0:T(128)} %bitcast.idx_ref, bf16[768,8192]{1,0:T(8,128)(2,1)S(1)} %copy-done.2, bf16[2,768,256]{2,1,0:T(8,128)(2,1)} %copy-done.3, bf16[2,1024,256]{2,1,0:T(8,128)(2,1)} %copy-done.19, f32[8,128]{1,0:T(8,128)} %copy-done.29, f32[8,128]{1,0:T(8,128)} %copy-done.30), custom_call_target="tpu_custom_call" | custom-call | flops 805306368 | bytes 2097152 | tf_op jit(solution)/shard_map/merged_block/pallas_call | solution.py:346
  103.0 1.2 collective-permute-start.19
  104.7 1.0 copy-done.20
  105.7 3.5 %merged_block.5 = (bf16[1024,256]{1,0:T(8,128)(2,1)}, bf16[1024,256]{1,0:T(8,128)(2,1)}) custom-call(s32[1]{0:T(128)} %bitcast.idx_ref, bf16[768,8192]{1,0:T(8,128)(2,1)S(1)} %copy-done.2, bf16[2,768,256]{2,1,0:T(8,128)(2,1)} %copy-done.3, bf16[2,1024,256]{2,1,0:T(8,128)(2,1)} %copy-done.20, f32[8,128]{1,0:T(8,128)} %copy-done.29, f32[8,128]{1,0:T(8,128)} %copy-done.30), custom_call_target="tpu_custom_call" | custom-call | flops 805306368 | bytes 2097152 | tf_op jit(solution)/shard_map/merged_block/pallas_call | solution.py:346
  109.1 1.0 copy-done.21
  110.1 3.5 %merged_block.6 = (bf16[1024,256]{1,0:T(8,128)(2,1)}, bf16[1024,256]{1,0:T(8,128)(2,1)}) custom-call(s32[1]{0:T(128)} %bitcast.idx_ref, bf16[768,8192]{1,0:T(8,128)(2,1)S(1)} %copy-done.2, bf16[2,768,256]{2,1,0:T(8,128)(2,1)} %copy-done.3, bf16[2,1024,256]{2,1,0:T(8,128)(2,1)} %copy-done.21, f32[8,128]{1,0:T(8,128)} %copy-done.29, f32[8,128]{1,0:T(8,128)} %copy-done.30), custom_call_target="tpu_custom_call" | custom-call | flops 805306368 | bytes 2097152 | tf_op jit(solution)/shard_map/merged_block/pallas_call | solution.py:346
  113.6 3.6 %collective-permute-done.19 = bf16[1024,256]{1,0:T(8,128)(2,1)S(1)} collective-permute-done((bf16[1024,256]{1,0:T(8,128)(2,1)}, bf16[1024,256]{1,0:T(8,128)(2,1)S(1)}, u32[]{:S(2)}, u32[]{:S(2)}) %collective-permute-start.19) | collective-permute-done | bytes 524320 | tf_op jit(solution)/shard_map/ppermute | solution.py:475
  118.1 2.0 add_convert_fusion
  120.1 3.1 %gradient_block.7 = bf16[2,1024,256]{2,1,0:T(8,128)(2,1)} custom-call(s32[1]{0:T(128)} %bitcast.idx_ref, bf16[768,8192]{1,0:T(8,128)(2,1)S(1)} %copy-done.2, bf16[2,768,256]{2,1,0:T(8,128)(2,1)} %copy-done.3), custom_call_target="tpu_custom_call" | custom-call | flops 805306368 | bytes 2097152 | tf_op jit(solution)/shard_map/gradient_block/pallas_call | solution.py:346
  123.7 1.1 collective-permute-start.25
  124.8 1.0 collective-permute-start.24
  125.7 1.5 collective-permute-start.26
  127.2 1.0 copy-done.22
  128.2 3.8 %merged_block.7 = (f32[1024,256]{1,0:T(8,128)}, f32[1024,256]{1,0:T(8,128)}) custom-call(s32[1]{0:T(128)} %bitcast.idx_ref, bf16[768,8192]{1,0:T(8,128)(2,1)S(1)} %copy-done.2, bf16[2,768,256]{2,1,0:T(8,128)(2,1)} %copy-done.3, bf16[2,1024,256]{2,1,0:T(8,128)(2,1)} %copy-done.22, f32[8,128]{1,0:T(8,128)} %copy-done.29, f32[8,128]{1,0:T(8,128)} %copy-done.30), custom_call_target="tpu_custom_call" | custom-call | flops 805306368 | bytes 2097152 | tf_op jit(solution)/shard_map/merged_block/pallas_call | solution.py:346
  132.0 6.1 %collective-permute-done.23.refs_1_ = bf16[1024,256]{1,0:T(8,128)(2,1)S(1)} collective-permute-done((bf16[1024,256]{1,0:T(8,128)(2,1)}, bf16[1024,256]{1,0:T(8,128)(2,1)S(1)}, u32[]{:S(2)}, u32[]{:S(2)}) %collective-permute-start.23) | collective-permute-done | bytes 524320 | tf_op jit(solution)/shard_map/ppermute | solution.py:475
  138.7 10.5 %collective-permute-done.24.refs_2_ = bf16[1024,256]{1,0:T(8,128)(2,1)S(1)} collective-permute-done((bf16[1024,256]{1,0:T(8,128)(2,1)}, bf16[1024,256]{1,0:T(8,128)(2,1)S(1)}, u32[]{:S(2)}, u32[]{:S(2)}) %collective-permute-start.24) | collective-permute-done | bytes 524320 | tf_op jit(solution)/shard_map/ppermute | solution.py:475
  149.2 1.2 copy-done.4
  150.4 1.2 copy-done.5
  152.4 1.1 collective-permute-start.29
  153.5 1.3 collective-permute-start.30
  154.8 1.6 collective-permute-start.27
  156.3 2.0 collective-permute-done.27
  158.4 1.2 collective-permute-start.28
  159.6 3.3 %collective-permute-done.28 = f32[8,128]{1,0:T(8,128)S(1)} collective-permute-done((f32[8,128]{1,0:T(8,128)S(1)}, f32[8,128]{1,0:T(8,128)S(1)}, u32[]{:S(2)}, u32[]{:S(2)}) %collective-permute-start.28) | collective-permute-done | bytes 4128 | tf_op jit(solution)/shard_map/ppermute | solution.py:475
  162.9 3.0 %collective-permute-done.29.refs_8_ = bf16[1024,256]{1,0:T(8,128)(2,1)} collective-permute-done((bf16[1024,256]{1,0:T(8,128)(2,1)S(1)}, bf16[1024,256]{1,0:T(8,128)(2,1)}, u32[]{:S(2)}, u32[]{:S(2)}) %collective-permute-start.29) | collective-permute-done | bytes 524320 | tf_op jit(solution)/shard_map/ppermute | solution.py:475
  166.5 1.2 collective-permute-done.31
  167.6 1.0 collective-permute-start.32
  168.7 2.6 %collective-permute-done.32 = f32[8,128]{1,0:T(8,128)S(1)} collective-permute-done((f32[8,128]{1,0:T(8,128)S(1)}, f32[8,128]{1,0:T(8,128)S(1)}, u32[]{:S(2)}, u32[]{:S(2)}) %collective-permute-start.32) | collective-permute-done | bytes 4128 | tf_op jit(solution)/shard_map/ppermute | solution.py:475
  171.2 1.3 collective-permute-start.33
  173.3 1.0 collective-permute-start.40
  175.5 9.8 %collective-permute-done.38.refs_10_ = bf16[1024,256]{1,0:T(8,128)(2,1)} collective-permute-done((bf16[1024,256]{1,0:T(8,128)(2,1)S(1)}, bf16[1024,256]{1,0:T(8,128)(2,1)}, u32[]{:S(2)}, u32[]{:S(2)}) %collective-permute-start.38) | collective-permute-done | bytes 524320 | tf_op jit(solution)/shard_map/ppermute | solution.py:475
  186.2 1.3 collective-permute-start.36
  187.5 1.3 collective-permute-start.44
  189.2 5.9 %blend.4 = (bf16[2,8192,256]{2,1,0:T(8,128)(2,1)}, f32[8,128]{1,0:T(8,128)}, bf16[2,1024,256]{2,1,0:T(8,128)(2,1)}) custom-call(s32[1]{0:T(128)} %bitcast.idx_ref, s32[2]{0:T(128)} %call_exported.1.masks_ref, f32[8,128]{1,0:T(8,128)} %add.35.square_ref, bf16[1024,256]{1,0:T(8,128)(2,1)} %copy-done.18, bf16[1024,256]{1,0:T(8,128)(2,1)} %collective-permute-done.2.refs_1_, ...), custom_call_target="tpu_custom_call" | custom-call | flops 4194304 | bytes 8388608 | tf_op jit(solution)/shard_map/blend/pallas_call | solution.py:441
  195.2 8.6 %blend.5 = (bf16[2,8192,256]{2,1,0:T(8,128)(2,1)}, f32[8,128]{1,0:T(8,128)}) custom-call(s32[1]{0:T(128)} %bitcast.idx_ref, s32[4]{0:T(128)} %constant.25.clone.masks_ref, f32[8,128]{1,0:T(8,128)} %add.35.square_ref, bf16[1024,256]{1,0:T(8,128)(2,1)} %collective-permute-done.refs_2_.refs_0_, ...), custom_call_target="tpu_custom_call", output_to_operand_aliasing={{0}: (20, {})} | custom-call | flops 8388608 | bytes 16777216 | tf_op jit(solution)/shard_map/blend/pallas_call | solution.py:441
  204.3 1.2 slice.11
  205.5 4.8 %blend.6 = (bf16[2,8192,256]{2,1,0:T(8,128)(2,1)}, f32[8,128]{1,0:T(8,128)}) custom-call(s32[1]{0:T(128)} %bitcast.idx_ref, s32[1]{0:T(128)} %constant.26.clone.masks_ref, f32[8,128]{1,0:T(8,128)} %add.35.square_ref, bf16[1024,256]{1,0:T(8,128)(2,1)} %collective-permute-done.1.refs_0_, ...), custom_call_target="tpu_custom_call", output_to_operand_aliasing={{0}: (8, {})} | custom-call | flops 2097152 | bytes 4194304 | tf_op jit(solution)/shard_map/blend/pallas_call | solution.py:441
  211.3 4.8 %blend.7 = (bf16[2,8192,256]{2,1,0:T(8,128)(2,1)}, f32[8,128]{1,0:T(8,128)}) custom-call(s32[1]{0:T(128)} %bitcast.idx_ref, s32[1]{0:T(128)} %constant.27.clone.masks_ref, f32[8,128]{1,0:T(8,128)} %add.35.square_ref, bf16[1024,256]{1,0:T(8,128)(2,1)} %collective-permute-done.11.refs_1_.refs_0_, ...), custom_call_target="tpu_custom_call", output_to_operand_aliasing={{0}: (8, {})} | custom-call | flops 2097152 | bytes 4194304 | tf_op jit(solution)/shard_map/blend/pallas_call | solution.py:441
  (121 shorter events, 15.3 us)
Async XLA Ops:
  2.7 21.5 %copy-start.18 = (bf16[1024,256]{1,0:T(8,128)(2,1)}, bf16[1024,256]{1,0:T(8,128)(2,1)S(1)}, u32[]{:S(2)}) copy-start(bf16[1024,256]{1,0:T(8,128)(2,1)S(1)} %get-tuple-element.106.refs_0_) | copy-start | bytes 1572868
  2.7 26.1 %collective-permute-start = (bf16[1024,256]{1,0:T(8,128)(2,1)S(1)}, bf16[1024,256]{1,0:T(8,128)(2,1)}, u32[]{:S(2)}, u32[]{:S(2)}) collective-permute-start(bf16[1024,256]{1,0:T(8,128)(2,1)S(1)} %get-tuple-element.106.refs_0_), channel_id=1, source_target_pairs={{0,8},{4,12},{8,0},{12,4},{16,24},{20,28},{24,16},{28,20},{1,9},{5... | collective-permute-start | bytes 1572872 | tf_op jit(solution)/shard_map/ppermute | solution.py:475
  5.7 25.7 %collective-permute-start.2 = (bf16[1024,256]{1,0:T(8,128)(2,1)S(1)}, bf16[1024,256]{1,0:T(8,128)(2,1)}, u32[]{:S(2)}, u32[]{:S(2)}) collective-permute-start(bf16[1024,256]{1,0:T(8,128)(2,1)S(1)} %get-tuple-element.106.refs_0_), channel_id=1, source_target_pairs={{0,4},{4,0},{8,12},{12,8},{16,20},{20,16},{24,28},{28,24},{1,5},{5... | collective-permute-start | bytes 1572872 | tf_op jit(solution)/shard_map/ppermute | solution.py:475
  5.7 23.2 %collective-permute-start.4 = (bf16[1024,256]{1,0:T(8,128)(2,1)S(1)}, bf16[1024,256]{1,0:T(8,128)(2,1)}, u32[]{:S(2)}, u32[]{:S(2)}) collective-permute-start(bf16[1024,256]{1,0:T(8,128)(2,1)S(1)} %get-tuple-element.106.refs_0_), channel_id=1, source_target_pairs={{0,16},{4,20},{8,24},{12,28},{16,0},{20,4},{24,8},{28,12},{1,17},{... | collective-permute-start | bytes 1572872 | tf_op jit(solution)/shard_map/ppermute | solution.py:475
  7.2 27.0 %copy-start.10 = (bf16[768,1024]{1,0:T(8,128)(2,1)S(1)}, bf16[768,1024]{1,0:T(8,128)(2,1)}, u32[]{:S(2)}) copy-start(bf16[768,1024]{1,0:T(8,128)(2,1)} %q_ref.2) | copy-start | bytes 4718596
  7.2 27.0 %copy-start.12 = (bf16[768,1024]{1,0:T(8,128)(2,1)S(1)}, bf16[768,1024]{1,0:T(8,128)(2,1)}, u32[]{:S(2)}) copy-start(bf16[768,1024]{1,0:T(8,128)(2,1)} %ro_ref.3) | copy-start | bytes 4718596
  7.2 27.0 %copy-start.15 = (s32[2]{0:T(128)S(1)}, s32[2]{0:T(128)}, u32[]{:S(2)}) copy-start(s32[2]{0:T(128)} %len_ref.3) | copy-start | bytes 28
  7.2 22.2 %collective-permute-start.7 = (bf16[1024,256]{1,0:T(8,128)(2,1)}, bf16[1024,256]{1,0:T(8,128)(2,1)}, u32[]{:S(2)}, u32[]{:S(2)}) collective-permute-start(bf16[1024,256]{1,0:T(8,128)(2,1)} %get-tuple-element.105.refs_6_.refs_2_), channel_id=1, source_target_pairs={{0,8},{4,12},{8,0},{12,4},{16,24},{20,28},{24,16},{28,20},{1,9},{5... | collective-permute-start | bytes 1572872 | tf_op jit(solution)/shard_map/ppermute | solution.py:475
  7.7 23.6 %collective-permute-start.9 = (bf16[1024,256]{1,0:T(8,128)(2,1)}, bf16[1024,256]{1,0:T(8,128)(2,1)}, u32[]{:S(2)}, u32[]{:S(2)}) collective-permute-start(bf16[1024,256]{1,0:T(8,128)(2,1)} %get-tuple-element.105.refs_6_.refs_2_), channel_id=1, source_target_pairs={{0,16},{4,20},{8,24},{12,28},{16,0},{20,4},{24,8},{28,12},{1,17},{... | collective-permute-start | bytes 1572872 | tf_op jit(solution)/shard_map/ppermute | solution.py:475
  24.2 4.6 %copy-start = (bf16[768,8192]{1,0:T(8,128)(2,1)}, bf16[768,8192]{1,0:T(8,128)(2,1)S(1)}, u32[]{:S(2)}) copy-start(bf16[768,8192]{1,0:T(8,128)(2,1)S(1)} %get-tuple-element.54.x_ref) | copy-start | bytes 37748740
  28.8 3.0 %collective-permute-start.6 = (bf16[1024,256]{1,0:T(8,128)(2,1)}, bf16[1024,256]{1,0:T(8,128)(2,1)}, u32[]{:S(2)}, u32[]{:S(2)}) collective-permute-start(bf16[1024,256]{1,0:T(8,128)(2,1)} %get-tuple-element.105.refs_6_.refs_2_), channel_id=1, source_target_pairs={{0,4},{4,0},{8,12},{12,8},{16,20},{20,16},{24,28},{28,24},{1,5},{5... | collective-permute-start | bytes 1572872 | tf_op jit(solution)/shard_map/ppermute | solution.py:475
  28.8 4.5 %collective-permute-start.3 = (bf16[1024,256]{1,0:T(8,128)(2,1)}, bf16[1024,256]{1,0:T(8,128)(2,1)}, u32[]{:S(2)}, u32[]{:S(2)}) collective-permute-start(bf16[1024,256]{1,0:T(8,128)(2,1)} %collective-permute-done.refs_2_.refs_0_), channel_id=1, source_target_pairs={{0,4},{4,0},{8,12},{12,8},{16,20},{20,16},{24,28},{28,24},{1,5},{5... | collective-permute-start | bytes 1572872 | tf_op jit(solution)/shard_map/ppermute | solution.py:475
  29.4 11.7 %collective-permute-start.5 = (bf16[1024,256]{1,0:T(8,128)(2,1)}, bf16[1024,256]{1,0:T(8,128)(2,1)}, u32[]{:S(2)}, u32[]{:S(2)}) collective-permute-start(bf16[1024,256]{1,0:T(8,128)(2,1)} %collective-permute-done.4.refs_4_.refs_2_), channel_id=1, source_target_pairs={{0,4},{4,0},{8,12},{12,8},{16,20},{20,16},{24,28},{28,24},{1,5},{5... | collective-permute-start | bytes 1572872 | tf_op jit(solution)/shard_map/ppermute | solution.py:475
  31.3 9.7 %collective-permute-start.8 = (bf16[1024,256]{1,0:T(8,128)(2,1)}, bf16[1024,256]{1,0:T(8,128)(2,1)}, u32[]{:S(2)}, u32[]{:S(2)}) collective-permute-start(bf16[1024,256]{1,0:T(8,128)(2,1)} %collective-permute-done.7.refs_8_.refs_4_), channel_id=1, source_target_pairs={{0,4},{4,0},{8,12},{12,8},{16,20},{20,16},{24,28},{28,24},{1,5},{5... | collective-permute-start | bytes 1572872 | tf_op jit(solution)/shard_map/ppermute | solution.py:475
  31.3 9.7 %collective-permute-start.10 = (bf16[1024,256]{1,0:T(8,128)(2,1)}, bf16[1024,256]{1,0:T(8,128)(2,1)}, u32[]{:S(2)}, u32[]{:S(2)}) collective-permute-start(bf16[1024,256]{1,0:T(8,128)(2,1)} %collective-permute-done.9.refs_10_.refs_6_), channel_id=1, source_target_pairs={{0,4},{4,0},{8,12},{12,8},{16,20},{20,16},{24,28},{28,24},{1,5},{5... | collective-permute-start | bytes 1572872 | tf_op jit(solution)/shard_map/ppermute | solution.py:475
  31.8 22.8 %collective-permute-start.1 = (bf16[1024,256]{1,0:T(8,128)(2,1)}, bf16[1024,256]{1,0:T(8,128)(2,1)}, u32[]{:S(2)}, u32[]{:S(2)}) collective-permute-start(bf16[1024,256]{1,0:T(8,128)(2,1)} %collective-permute-done.refs_2_.refs_0_), channel_id=1, source_target_pairs={{0,16},{4,20},{8,24},{12,28},{16,0},{20,4},{24,8},{28,12},{1,17},{... | collective-permute-start | bytes 1572872 | tf_op jit(solution)/shard_map/ppermute | solution.py:475
  33.4 21.4 %collective-permute-start.12 = (bf16[1024,256]{1,0:T(8,128)(2,1)}, bf16[1024,256]{1,0:T(8,128)(2,1)}, u32[]{:S(2)}, u32[]{:S(2)}) collective-permute-start(bf16[1024,256]{1,0:T(8,128)(2,1)} %collective-permute-done.9.refs_10_.refs_6_), channel_id=1, source_target_pairs={{0,8},{4,12},{8,0},{12,4},{16,24},{20,28},{24,16},{28,20},{1,9},{5... | collective-permute-start | bytes 1572872 | tf_op jit(solution)/shard_map/ppermute | solution.py:475
  41.6 4.6 %copy-start.1 = (bf16[768,8192]{1,0:T(8,128)(2,1)S(1)}, bf16[768,8192]{1,0:T(8,128)(2,1)}, u32[]{:S(2)}) copy-start(bf16[768,8192]{1,0:T(8,128)(2,1)} %copy-done) | copy-start | bytes 37748740
  54.6 8.7 %copy-start.8 = (f32[384,128]{1,0:T(8,128)S(1)}, f32[384,128]{1,0:T(8,128)}, u32[]{:S(2)}) copy-start(f32[384,128]{1,0:T(8,128)} %constant.22.clone.cos_ref.refs_5_.rest_1_) | copy-start | bytes 589828
  54.6 8.7 %copy-start.9 = (f32[384,128]{1,0:T(8,128)S(1)}, f32[384,128]{1,0:T(8,128)}, u32[]{:S(2)}) copy-start(f32[384,128]{1,0:T(8,128)} %constant.23.clone.sin_ref.refs_6_.rest_2_) | copy-start | bytes 589828
  54.6 8.7 %copy-start.11 = (bf16[768,1024]{1,0:T(8,128)(2,1)S(1)}, bf16[768,1024]{1,0:T(8,128)(2,1)}, u32[]{:S(2)}) copy-start(bf16[768,1024]{1,0:T(8,128)(2,1)} %q_ref.3) | copy-start | bytes 4718596
  54.6 2.3 %collective-permute-start.11 = (bf16[1024,256]{1,0:T(8,128)(2,1)}, bf16[1024,256]{1,0:T(8,128)(2,1)}, u32[]{:S(2)}, u32[]{:S(2)}) collective-permute-start(bf16[1024,256]{1,0:T(8,128)(2,1)} %collective-permute-done.1.refs_0_), channel_id=1, source_target_pairs={{0,4},{4,0},{8,12},{12,8},{16,20},{20,16},{24,28},{28,24},{1,5},{5... | collective-permute-start | bytes 1572872 | tf_op jit(solution)/shard_map/ppermute | solution.py:475
  54.7 3.0 %collective-permute-start.13 = (bf16[1024,256]{1,0:T(8,128)(2,1)}, bf16[1024,256]{1,0:T(8,128)(2,1)}, u32[]{:S(2)}, u32[]{:S(2)}) collective-permute-start(bf16[1024,256]{1,0:T(8,128)(2,1)} %collective-permute-done.12.refs_2_.refs_1_), channel_id=1, source_target_pairs={{0,4},{4,0},{8,12},{12,8},{16,20},{20,16},{24,28},{28,24},{1,5},{5... | collective-permute-start | bytes 1572872 | tf_op jit(solution)/shard_map/ppermute | solution.py:475
  75.0 4.6 %copy-start.2 = (bf16[768,8192]{1,0:T(8,128)(2,1)S(1)}, bf16[768,8192]{1,0:T(8,128)(2,1)}, u32[]{:S(2)}) copy-start(bf16[768,8192]{1,0:T(8,128)(2,1)} %copy-done) | copy-start | bytes 37748740
  82.7 15.3 %collective-permute-start.17 = (bf16[2,1024,256]{2,1,0:T(8,128)(2,1)}, bf16[2,1024,256]{2,1,0:T(8,128)(2,1)S(1)}, u32[]{:S(2)}, u32[]{:S(2)}) collective-permute-start(bf16[2,1024,256]{2,1,0:T(8,128)(2,1)} %gradient_block.4), channel_id=1, source_target_pairs={{0,4},{4,0},{8,12},{12,8},{16,20},{20,16},{24,28},{28,24},{1,5},{5... | collective-permute-start | bytes 3145736 | tf_op jit(solution)/shard_map/ppermute | solution.py:475
  82.8 3.6 %collective-permute-start.14 = (f32[8,128]{1,0:T(8,128)S(1)}, f32[8,128]{1,0:T(8,128)S(1)}, u32[]{:S(2)}, u32[]{:S(2)}) collective-permute-start(f32[8,128]{1,0:T(8,128)S(1)} %get-tuple-element.66), channel_id=1, source_target_pairs={{0,1},{1,0},{2,3},{3,2},{4,5},{5,4},{6,7},{7,6},{8,9},{9,8},{10,11... | collective-permute-start | bytes 12296 | tf_op jit(solution)/shard_map/ppermute | solution.py:475
  86.4 5.7 %collective-permute-start.15 = (f32[8,128]{1,0:T(8,128)S(1)}, f32[8,128]{1,0:T(8,128)S(1)}, u32[]{:S(2)}, u32[]{:S(2)}) collective-permute-start(f32[8,128]{1,0:T(8,128)S(1)} %add.27), channel_id=1, source_target_pairs={{0,2},{1,3},{2,0},{3,1},{4,6},{5,7},{6,4},{7,5},{8,10},{9,11},{10,... | collective-permute-start | bytes 12296 | tf_op jit(solution)/shard_map/ppermute | solution.py:475
  92.2 12.6 %collective-permute-start.18 = (bf16[2,1024,256]{2,1,0:T(8,128)(2,1)}, bf16[2,1024,256]{2,1,0:T(8,128)(2,1)S(1)}, u32[]{:S(2)}, u32[]{:S(2)}) collective-permute-start(bf16[2,1024,256]{2,1,0:T(8,128)(2,1)} %gradient_block.5), channel_id=1, source_target_pairs={{0,4},{4,0},{8,12},{12,8},{16,20},{20,16},{24,28},{28,24},{1,5},{5... | collective-permute-start | bytes 3145736 | tf_op jit(solution)/shard_map/ppermute | solution.py:475
  92.2 5.8 %copy-start.29 = (f32[8,128]{1,0:T(8,128)}, f32[8,128]{1,0:T(8,128)S(1)}, u32[]{:S(2)}) copy-start(f32[8,128]{1,0:T(8,128)S(1)} %add.28.mine_margin) | copy-start | bytes 12292
  95.3 13.8 %collective-permute-start.20 = (bf16[2,1024,256]{2,1,0:T(8,128)(2,1)}, bf16[2,1024,256]{2,1,0:T(8,128)(2,1)S(1)}, u32[]{:S(2)}, u32[]{:S(2)}) collective-permute-start(bf16[2,1024,256]{2,1,0:T(8,128)(2,1)} %gradient_block.6), channel_id=1, source_target_pairs={{0,4},{4,0},{8,12},{12,8},{16,20},{20,16},{24,28},{28,24},{1,5},{5... | collective-permute-start | bytes 3145736 | tf_op jit(solution)/shard_map/ppermute | solution.py:475
  95.8 2.2 %collective-permute-start.16 = (f32[8,128]{1,0:T(8,128)S(1)}, f32[8,128]{1,0:T(8,128)S(1)}, u32[]{:S(2)}, u32[]{:S(2)}) collective-permute-start(f32[8,128]{1,0:T(8,128)S(1)} %add.28.mine_margin), channel_id=1, source_target_pairs={{0,4},{4,0},{8,12},{12,8},{16,20},{20,16},{24,28},{28,24},{1,5},{5... | collective-permute-start | bytes 12296 | tf_op jit(solution)/shard_map/ppermute | solution.py:475
  103.0 14.2 %collective-permute-start.19 = (bf16[1024,256]{1,0:T(8,128)(2,1)}, bf16[1024,256]{1,0:T(8,128)(2,1)S(1)}, u32[]{:S(2)}, u32[]{:S(2)}) collective-permute-start(bf16[1024,256]{1,0:T(8,128)(2,1)} %get-tuple-element.76), channel_id=1, source_target_pairs={{0,8},{4,12},{8,0},{12,4},{16,24},{20,28},{24,16},{28,20},{1,9},{5... | collective-permute-start | bytes 1572872 | tf_op jit(solution)/shard_map/ppermute | solution.py:475
  104.2 13.9 %collective-permute-start.21 = (bf16[1024,256]{1,0:T(8,128)(2,1)}, bf16[1024,256]{1,0:T(8,128)(2,1)S(1)}, u32[]{:S(2)}, u32[]{:S(2)}) collective-permute-start(bf16[1024,256]{1,0:T(8,128)(2,1)} %get-tuple-element.75), channel_id=1, source_target_pairs={{0,16},{4,20},{8,24},{12,28},{16,0},{20,4},{24,8},{28,12},{1,17},{... | collective-permute-start | bytes 1572872 | tf_op jit(solution)/shard_map/ppermute | solution.py:475
  109.1 8.0 %copy-start.28 = (bf16[1024,256]{1,0:T(8,128)(2,1)S(1)}, bf16[1024,256]{1,0:T(8,128)(2,1)}, u32[]{:S(2)}) copy-start(bf16[1024,256]{1,0:T(8,128)(2,1)} %get-tuple-element.78) | copy-start | bytes 1572868
  123.2 4.1 %collective-permute-start.22 = (bf16[2,1024,256]{2,1,0:T(8,128)(2,1)}, bf16[2,1024,256]{2,1,0:T(8,128)(2,1)S(1)}, u32[]{:S(2)}, u32[]{:S(2)}) collective-permute-start(bf16[2,1024,256]{2,1,0:T(8,128)(2,1)} %gradient_block.7), channel_id=1, source_target_pairs={{0,4},{4,0},{8,12},{12,8},{16,20},{20,16},{24,28},{28,24},{1,5},{5... | collective-permute-start | bytes 3145736 | tf_op jit(solution)/shard_map/ppermute | solution.py:475
  123.2 14.9 %collective-permute-start.23 = (bf16[1024,256]{1,0:T(8,128)(2,1)}, bf16[1024,256]{1,0:T(8,128)(2,1)S(1)}, u32[]{:S(2)}, u32[]{:S(2)}) collective-permute-start(bf16[1024,256]{1,0:T(8,128)(2,1)} %get-tuple-element.79), channel_id=1, source_target_pairs={{0,16},{4,20},{8,24},{12,28},{16,0},{20,4},{24,8},{28,12},{1,17},{... | collective-permute-start | bytes 1572872 | tf_op jit(solution)/shard_map/ppermute | solution.py:475
  123.7 15.0 %collective-permute-start.25 = (bf16[1024,256]{1,0:T(8,128)(2,1)}, bf16[1024,256]{1,0:T(8,128)(2,1)S(1)}, u32[]{:S(2)}, u32[]{:S(2)}) collective-permute-start(bf16[1024,256]{1,0:T(8,128)(2,1)} %get-tuple-element.86), channel_id=1, source_target_pairs={{0,8},{4,12},{8,0},{12,4},{16,24},{20,28},{24,16},{28,20},{1,9},{5... | collective-permute-start | bytes 1572872 | tf_op jit(solution)/shard_map/ppermute | solution.py:475
  124.8 24.4 %collective-permute-start.24 = (bf16[1024,256]{1,0:T(8,128)(2,1)}, bf16[1024,256]{1,0:T(8,128)(2,1)S(1)}, u32[]{:S(2)}, u32[]{:S(2)}) collective-permute-start(bf16[1024,256]{1,0:T(8,128)(2,1)} %add_convert_fusion), channel_id=1, source_target_pairs={{0,8},{4,12},{8,0},{12,4},{16,24},{20,28},{24,16},{28,20},{1,9},{5... | collective-permute-start | bytes 1572872 | tf_op jit(solution)/shard_map/ppermute | solution.py:475
  125.7 23.5 %collective-permute-start.26 = (bf16[1024,256]{1,0:T(8,128)(2,1)S(1)}, bf16[1024,256]{1,0:T(8,128)(2,1)S(1)}, u32[]{:S(2)}, u32[]{:S(2)}) collective-permute-start(bf16[1024,256]{1,0:T(8,128)(2,1)S(1)} %add_convert_fusion.1), channel_id=1, source_target_pairs={{0,16},{4,20},{8,24},{12,28},{16,0},{20,4},{24,8},{28,12},{1,17},{... | collective-permute-start | bytes 1572872 | tf_op jit(solution)/shard_map/ppermute | solution.py:475
  149.2 1.2 copy-start.4
  152.3 36.9 %copy-start.6 = (bf16[1024,256]{1,0:T(8,128)(2,1)}, bf16[1024,256]{1,0:T(8,128)(2,1)S(1)}, u32[]{:S(2)}) copy-start(bf16[1024,256]{1,0:T(8,128)(2,1)S(1)} %get-tuple-element.88.refs_4_) | copy-start | bytes 1572868
  152.3 36.9 %copy-start.7 = (bf16[1024,256]{1,0:T(8,128)(2,1)}, bf16[1024,256]{1,0:T(8,128)(2,1)S(1)}, u32[]{:S(2)}) copy-start(bf16[1024,256]{1,0:T(8,128)(2,1)S(1)} %get-tuple-element.89.refs_6_) | copy-start | bytes 1572868
  152.4 13.5 %collective-permute-start.29 = (bf16[1024,256]{1,0:T(8,128)(2,1)S(1)}, bf16[1024,256]{1,0:T(8,128)(2,1)}, u32[]{:S(2)}, u32[]{:S(2)}) collective-permute-start(bf16[1024,256]{1,0:T(8,128)(2,1)S(1)} %get-tuple-element.88.refs_4_), channel_id=1, source_target_pairs={{0,8},{4,12},{8,0},{12,4},{16,24},{20,28},{24,16},{28,20},{1,9},{5... | collective-permute-start | bytes 1572872 | tf_op jit(solution)/shard_map/ppermute | solution.py:475
  153.5 13.0 %collective-permute-start.30 = (bf16[1024,256]{1,0:T(8,128)(2,1)S(1)}, bf16[1024,256]{1,0:T(8,128)(2,1)S(1)}, u32[]{:S(2)}, u32[]{:S(2)}) collective-permute-start(bf16[1024,256]{1,0:T(8,128)(2,1)S(1)} %get-tuple-element.89.refs_6_), channel_id=1, source_target_pairs={{0,16},{4,20},{8,24},{12,28},{16,0},{20,4},{24,8},{28,12},{1,17},{... | collective-permute-start | bytes 1572872 | tf_op jit(solution)/shard_map/ppermute | solution.py:475
  154.8 3.6 %collective-permute-start.27 = (f32[8,128]{1,0:T(8,128)S(1)}, f32[8,128]{1,0:T(8,128)S(1)}, u32[]{:S(2)}, u32[]{:S(2)}) collective-permute-start(f32[8,128]{1,0:T(8,128)S(1)} %get-tuple-element.87), channel_id=1, source_target_pairs={{0,1},{1,0},{2,3},{3,2},{4,5},{5,4},{6,7},{7,6},{8,9},{9,8},{10,11... | collective-permute-start | bytes 12296 | tf_op jit(solution)/shard_map/ppermute | solution.py:475
  158.4 4.5 %collective-permute-start.28 = (f32[8,128]{1,0:T(8,128)S(1)}, f32[8,128]{1,0:T(8,128)S(1)}, u32[]{:S(2)}, u32[]{:S(2)}) collective-permute-start(f32[8,128]{1,0:T(8,128)S(1)} %add.31), channel_id=1, source_target_pairs={{0,2},{1,3},{2,0},{3,1},{4,6},{5,7},{6,4},{7,5},{8,10},{9,11},{10,... | collective-permute-start | bytes 12296 | tf_op jit(solution)/shard_map/ppermute | solution.py:475
  166.4 28.7 %copy-start.23 = (bf16[1024,256]{1,0:T(8,128)(2,1)}, bf16[1024,256]{1,0:T(8,128)(2,1)S(1)}, u32[]{:S(2)}) copy-start(bf16[1024,256]{1,0:T(8,128)(2,1)S(1)} %collective-permute-done.30.refs_14_) | copy-start | bytes 1572868
  166.4 1.2 collective-permute-start.31
  167.6 3.6 %collective-permute-start.32 = (f32[8,128]{1,0:T(8,128)S(1)}, f32[8,128]{1,0:T(8,128)S(1)}, u32[]{:S(2)}, u32[]{:S(2)}) collective-permute-start(f32[8,128]{1,0:T(8,128)S(1)} %add.33), channel_id=1, source_target_pairs={{0,8},{4,12},{8,0},{12,4},{16,24},{20,28},{24,16},{28,20},{1,9},{5... | collective-permute-start | bytes 12296 | tf_op jit(solution)/shard_map/ppermute | solution.py:475
  171.2 3.6 %collective-permute-start.33 = (f32[8,128]{1,0:T(8,128)S(1)}, f32[8,128]{1,0:T(8,128)S(1)}, u32[]{:S(2)}, u32[]{:S(2)}) collective-permute-start(f32[8,128]{1,0:T(8,128)S(1)} %add.34), channel_id=1, source_target_pairs={{0,16},{4,20},{8,24},{12,28},{16,0},{20,4},{24,8},{28,12},{1,17},{... | collective-permute-start | bytes 12296 | tf_op jit(solution)/shard_map/ppermute | solution.py:475
  172.5 12.7 %collective-permute-start.38 = (bf16[1024,256]{1,0:T(8,128)(2,1)S(1)}, bf16[1024,256]{1,0:T(8,128)(2,1)}, u32[]{:S(2)}, u32[]{:S(2)}) collective-permute-start(bf16[1024,256]{1,0:T(8,128)(2,1)S(1)} %get-tuple-element.88.refs_4_), channel_id=1, source_target_pairs={{0,16},{4,20},{8,24},{12,28},{16,0},{20,4},{24,8},{28,12},{1,17},{... | collective-permute-start | bytes 1572872 | tf_op jit(solution)/shard_map/ppermute | solution.py:475
  173.3 12.4 %collective-permute-start.40 = (bf16[1024,256]{1,0:T(8,128)(2,1)S(1)}, bf16[1024,256]{1,0:T(8,128)(2,1)}, u32[]{:S(2)}, u32[]{:S(2)}) collective-permute-start(bf16[1024,256]{1,0:T(8,128)(2,1)S(1)} %get-tuple-element.89.refs_6_), channel_id=1, source_target_pairs={{0,8},{4,12},{8,0},{12,4},{16,24},{20,28},{24,16},{28,20},{1,9},{5... | collective-permute-start | bytes 1572872 | tf_op jit(solution)/shard_map/ppermute | solution.py:475
  174.3 11.4 %collective-permute-start.34 = (bf16[1024,256]{1,0:T(8,128)(2,1)S(1)}, bf16[1024,256]{1,0:T(8,128)(2,1)S(1)}, u32[]{:S(2)}, u32[]{:S(2)}) collective-permute-start(bf16[1024,256]{1,0:T(8,128)(2,1)S(1)} %get-tuple-element.88.refs_4_), channel_id=1, source_target_pairs={{0,4},{4,0},{8,12},{12,8},{16,20},{20,16},{24,28},{28,24},{1,5},{5... | collective-permute-start | bytes 1572872 | tf_op jit(solution)/shard_map/ppermute | solution.py:475
  174.3 11.9 %collective-permute-start.35 = (bf16[1024,256]{1,0:T(8,128)(2,1)S(1)}, bf16[1024,256]{1,0:T(8,128)(2,1)S(1)}, u32[]{:S(2)}, u32[]{:S(2)}) collective-permute-start(bf16[1024,256]{1,0:T(8,128)(2,1)S(1)} %get-tuple-element.89.refs_6_), channel_id=1, source_target_pairs={{0,4},{4,0},{8,12},{12,8},{16,20},{20,16},{24,28},{28,24},{1,5},{5... | collective-permute-start | bytes 1572872 | tf_op jit(solution)/shard_map/ppermute | solution.py:475
  175.5 12.0 %collective-permute-start.37 = (bf16[1024,256]{1,0:T(8,128)(2,1)}, bf16[1024,256]{1,0:T(8,128)(2,1)}, u32[]{:S(2)}, u32[]{:S(2)}) collective-permute-start(bf16[1024,256]{1,0:T(8,128)(2,1)} %collective-permute-done.29.refs_8_), channel_id=1, source_target_pairs={{0,4},{4,0},{8,12},{12,8},{16,20},{20,16},{24,28},{28,24},{1,5},{5... | collective-permute-start | bytes 1572872 | tf_op jit(solution)/shard_map/ppermute | solution.py:475
  185.2 9.9 %collective-permute-start.39 = (bf16[1024,256]{1,0:T(8,128)(2,1)}, bf16[1024,256]{1,0:T(8,128)(2,1)}, u32[]{:S(2)}, u32[]{:S(2)}) collective-permute-start(bf16[1024,256]{1,0:T(8,128)(2,1)} %collective-permute-done.38.refs_10_), channel_id=1, source_target_pairs={{0,4},{4,0},{8,12},{12,8},{16,20},{20,16},{24,28},{28,24},{1,5},{5... | collective-permute-start | bytes 1572872 | tf_op jit(solution)/shard_map/ppermute | solution.py:475
  185.7 9.5 %collective-permute-start.41 = (bf16[1024,256]{1,0:T(8,128)(2,1)}, bf16[1024,256]{1,0:T(8,128)(2,1)}, u32[]{:S(2)}, u32[]{:S(2)}) collective-permute-start(bf16[1024,256]{1,0:T(8,128)(2,1)} %collective-permute-done.40.refs_12_), channel_id=1, source_target_pairs={{0,4},{4,0},{8,12},{12,8},{16,20},{20,16},{24,28},{28,24},{1,5},{5... | collective-permute-start | bytes 1572872 | tf_op jit(solution)/shard_map/ppermute | solution.py:475
  185.7 1.7 copy-start.24
  185.8 9.4 %collective-permute-start.42 = (bf16[1024,256]{1,0:T(8,128)(2,1)S(1)}, bf16[1024,256]{1,0:T(8,128)(2,1)}, u32[]{:S(2)}, u32[]{:S(2)}) collective-permute-start(bf16[1024,256]{1,0:T(8,128)(2,1)S(1)} %collective-permute-done.30.refs_14_), channel_id=1, source_target_pairs={{0,4},{4,0},{8,12},{12,8},{16,20},{20,16},{24,28},{28,24},{1,5},{5... | collective-permute-start | bytes 1572872 | tf_op jit(solution)/shard_map/ppermute | solution.py:475
  186.2 1.3 copy-start.25
  186.2 17.6 %collective-permute-start.36 = (bf16[1024,256]{1,0:T(8,128)(2,1)}, bf16[1024,256]{1,0:T(8,128)(2,1)}, u32[]{:S(2)}, u32[]{:S(2)}) collective-permute-start(bf16[1024,256]{1,0:T(8,128)(2,1)} %collective-permute-done.29.refs_8_), channel_id=1, source_target_pairs={{0,16},{4,20},{8,24},{12,28},{16,0},{20,4},{24,8},{28,12},{1,17},{... | collective-permute-start | bytes 1572872 | tf_op jit(solution)/shard_map/ppermute | solution.py:475
  187.5 16.4 %collective-permute-start.44 = (bf16[1024,256]{1,0:T(8,128)(2,1)S(1)}, bf16[1024,256]{1,0:T(8,128)(2,1)}, u32[]{:S(2)}, u32[]{:S(2)}) collective-permute-start(bf16[1024,256]{1,0:T(8,128)(2,1)S(1)} %collective-permute-done.30.refs_14_), channel_id=1, source_target_pairs={{0,8},{4,12},{8,0},{12,4},{16,24},{20,28},{24,16},{28,20},{1,9},{5... | collective-permute-start | bytes 1572872 | tf_op jit(solution)/shard_map/ppermute | solution.py:475
  203.7 6.6 %collective-permute-start.43 = (bf16[1024,256]{1,0:T(8,128)(2,1)}, bf16[1024,256]{1,0:T(8,128)(2,1)S(1)}, u32[]{:S(2)}, u32[]{:S(2)}) collective-permute-start(bf16[1024,256]{1,0:T(8,128)(2,1)} %collective-permute-done.36.refs_2_), channel_id=1, source_target_pairs={{0,4},{4,0},{8,12},{12,8},{16,20},{20,16},{24,28},{28,24},{1,5},{5... | collective-permute-start | bytes 1572872 | tf_op jit(solution)/shard_map/ppermute | solution.py:475
  203.8 6.6 %collective-permute-start.45 = (bf16[1024,256]{1,0:T(8,128)(2,1)}, bf16[1024,256]{1,0:T(8,128)(2,1)S(1)}, u32[]{:S(2)}, u32[]{:S(2)}) collective-permute-start(bf16[1024,256]{1,0:T(8,128)(2,1)} %collective-permute-done.44.refs_3_), channel_id=1, source_target_pairs={{0,4},{4,0},{8,12},{12,8},{16,20},{20,16},{24,28},{28,24},{1,5},{5... | collective-permute-start | bytes 1572872 | tf_op jit(solution)/shard_map/ppermute | solution.py:475
  (13 other events, 12.3 us)
where the time goes:
time: 217 us; the launch traced here: 216 us
  Pallas kernels  95.5 us (44%)
  waiting for transfers between devices  53 us (24%)
  starting transfers between devices  33.1 us (15%)
  local copies, waits for them, and re-layouts  30.8 us (14%)
  other arithmetic  2.7 us (1%)
    ppermute x46, waiting for transfers between devices, swap(): return lax.ppermute(x, axis, [(i, i ^ bit) for i in range(size)])  53 us
    ppermute x46, starting transfers between devices, swap(): return lax.ppermute(x, axis, [(i, i ^ bit) for i in range(size)])  33.1 us
    pallas_call x8, Pallas kernels, gradient_block(): pl.pallas_call(functools.partial(kernel, mask), in_specs=[SMEM] + [VMEM]...  26.7 us
    unnamed x62, local copies, waits for them, and re-layouts  26.5 us
    pallas_call x4, Pallas kernels, blend(): pl.pallas_call(functools.partial(blend_kernel, count, first), in_specs=in...  24.1 us
    pallas_call x1, Pallas kernels, norm_project(): pl.pallas_call(norm_project_kernel, in_specs=[HBM, HBM, VMEM, VMEM], out_...  16.4 us
    pallas_call x2, Pallas kernels, project(): pl.pallas_call(functools.partial(project_kernel, count, first, last), in_...  14 us
    pallas_call x2, Pallas kernels, attend(): pl.pallas_call(functools.partial(attend_kernel, back), grid_spec=pltpu.Pr...  13.6 us
  transfers between devices with their start and end apart: 46, of which 19 were waited for; matrix products, arithmetic and copies ran while one was open for 1% of the time, Pallas kernels for 32%

commit v1 on v0

v1 whole, which is shorter than its diff:
```python
import functools
import math

import jax
import jax.numpy as jnp
import numpy as np
from jax import lax
from jax.experimental import pallas as pl
from jax.experimental.pallas import tpu as pltpu
from jax.sharding import PartitionSpec as P

D = 8192
HD = 128
KVH = 8
QH = 32
LEN = 384
TILE = 128

rope_base = 1000000.0
dpo_beta = 0.1
learning_rate = 0.2
mix_alpha = 0.6
norm_eps = 1e-06
width_scale = D ** (-0.5)
logit_scale = 1.0 / math.sqrt(HD)
MIB = 1024 * 1024

NT = (((1,), (1,)), ((), ()))
NN = (((1,), (0,)), ((), ()))
TN = (((0,), (0,)), ((), ()))


def dot(a, b, dims):
    return lax.dot_general(a, b, dims, preferred_element_type=jnp.float32)


def params(mib):
    return pltpu.CompilerParams(vmem_limit_bytes=mib * MIB)


COST = pl.CostEstimate(flops=1, bytes_accessed=1, transcendentals=0)
VMEM = pl.BlockSpec(memory_space=pltpu.VMEM)
SMEM = pl.BlockSpec(memory_space=pltpu.SMEM)
HBM = pl.BlockSpec(memory_space=pl.ANY)


def resident(x):
    return pltpu.with_memory_space_constraint(x, pltpu.VMEM)


def in_hbm(x):
    return pltpu.with_memory_space_constraint(x, pltpu.HBM)


def rope_tables():
    frequency = rope_base ** (-2.0 * np.arange(HD // 2) / HD)
    angles = np.arange(LEN)[:, None] * frequency[None, :]
    cosine, sine = np.cos(angles), np.sin(angles)
    return np.stack([np.concatenate([cosine, cosine], axis=1), np.concatenate([-sine, sine], axis=1)]).astype(np.float32)


def store_heads(acc_ref, cos, sin, key_ref, value_ref):
    for s in range(key_ref.shape[0] // LEN):
        rows = slice(s * LEN, (s + 1) * LEN)
        for h in range(key_ref.shape[1] // HD):
            cols = slice(h * HD, (h + 1) * HD)
            k = acc_ref[0, rows, cols] * width_scale
            key_ref[rows, cols] = (k * cos + pltpu.roll(k, HD // 2, 1) * sin).astype(jnp.bfloat16)
    value_ref[...] = (acc_ref[1] * width_scale).astype(jnp.bfloat16)


def norm_project_kernel(
    hidden_hbm, weight_hbm, table_hbm, normed_ref, key_ref, value_ref, x, w, acc, part, table, in_sem, w_sem, table_sem
):
    tokens = x.shape[0]
    step, width, span, chunk = 16, 512, 128, 1024
    reads = []
    for i in range(tokens // span):
        at = pl.ds(i * span, span)
        reads.append(pltpu.make_async_copy(hidden_hbm.at[at], x.at[at], in_sem.at[i]))
    loads = []
    for c in range(D // chunk):
        at = pl.ds(c * chunk, chunk)
        loads.append(pltpu.make_async_copy(weight_hbm.at[:, at, :], w.at[:, at, :], w_sem.at[c]))
    loads.append(pltpu.make_async_copy(table_hbm, table, table_sem))
    for copy in reads + loads:
        copy.start()

    def row_step(i, carry):
        at = pl.ds(pl.multiple_of(i * step, step), step)
        total = jnp.zeros((step, width), jnp.float32)
        for c in range(D // width):
            v = x[at, c * width : (c + 1) * width].astype(jnp.float32)
            total = total + v * v
        part[at, :] = functools.reduce(jnp.add, [total[:, c * 128 : (c + 1) * 128] for c in range(width // 128)])
        return carry

    for i, copy in enumerate(reads):
        copy.wait()
        lax.fori_loop(i * (span // step), (i + 1) * (span // step), row_step, 0)
    for copy in loads:
        copy.wait()
    mean = jnp.sum(part[...], axis=1, keepdims=True) * (1.0 / D)
    part[...] = jnp.broadcast_to(lax.rsqrt(mean + norm_eps), part.shape)

    def normalise(c):
        at = slice(c * chunk, (c + 1) * chunk)
        for i in range(tokens // step):
            rows = slice(i * step, (i + 1) * step)
            scale = jnp.concatenate([part[rows, :]] * (chunk // 128), axis=1)
            normed_ref[rows, at] = (x[rows, at].astype(jnp.float32) * scale).astype(jnp.bfloat16)

    normalise(0)
    for c in range(D // chunk):
        at = slice(c * chunk, (c + 1) * chunk)
        for i in (0, 1):
            term = dot(normed_ref[:, at], w[i, at, :], NN)
            acc[i] = term if c == 0 else acc[i] + term
        if (c + 1) * chunk < D:
            normalise(c + 1)
    store_heads(acc, table[0], table[1], key_ref, value_ref)


def norm_project(hidden, weights, tables):
    tokens = hidden.shape[0]
    cols = weights.shape[2]
    return pl.pallas_call(
        norm_project_kernel,
        in_specs=[HBM, HBM, HBM],
        out_specs=[VMEM, VMEM, VMEM],
        out_shape=[
            pltpu.VMEM((tokens, D), jnp.bfloat16),
            pltpu.VMEM((tokens, cols), jnp.bfloat16),
            pltpu.VMEM((tokens, cols), jnp.bfloat16),
        ],
        scratch_shapes=[
            pltpu.VMEM((tokens, D), jnp.bfloat16),
            pltpu.VMEM((2, D, cols), jnp.bfloat16),
            pltpu.VMEM((2, tokens, cols), jnp.float32),
            pltpu.VMEM((tokens, 128), jnp.float32),
            pltpu.VMEM(tables.shape, jnp.float32),
            pltpu.SemaphoreType.DMA((tokens // 128,)),
            pltpu.SemaphoreType.DMA((D // 1024,)),
            pltpu.SemaphoreType.DMA,
        ],
        compiler_params=params(29),
        cost_estimate=COST,
        name="norm_project",
    )(in_hbm(hidden), in_hbm(weights), in_hbm(tables))


def project_kernel(masks, first, last, idx_ref, x_ref, *refs):
    refs = list(refs)
    count = len(masks)
    pieces = [refs[:count], refs[count : 2 * count]]
    refs = refs[2 * count :]
    held = None if first else refs.pop(0)
    if last:
        table_hbm, key_ref, value_ref, w, acc, table, sem, table_sem = refs
        table_copy = pltpu.make_async_copy(table_hbm, table, table_sem)
        table_copy.start()
    else:
        acc, w, sem = refs
    depth = w.shape[2]
    copies = [[pltpu.make_async_copy(pieces[i][n], w.at[i, n], sem.at[i, n]) for i in (0, 1)] for n in range(count)]
    for pair in copies:
        for copy in pair:
            copy.start()
    for n in range(count):
        for copy in copies[n]:
            copy.wait()
        col = pl.multiple_of((idx_ref[0] ^ masks[n]) * depth, depth)
        x = x_ref[:, pl.ds(col, depth)]
        for i in (0, 1):
            term = dot(x, w[i, n], NN)
            if n:
                term = acc[i] + term
            elif not first:
                term = held[i] + term
            acc[i] = term
    if last:
        table_copy.wait()
        store_heads(acc, table[0], table[1], key_ref, value_ref)


def project(idx, normed, masks, pieces, held, tables):
    tokens = normed.shape[0]
    rows, cols = pieces[masks[0]][0].shape
    first, last = held is None, tables is not None
    count = len(masks)
    in_specs = [SMEM, VMEM] + [HBM] * (2 * count)
    args = [idx, resident(normed)]
    args += [pieces[m][i] for i in (0, 1) for m in masks]
    if not first:
        in_specs.append(VMEM)
        args.append(resident(held))
    acc_shape = (2, tokens, cols)
    scratch = [pltpu.VMEM((2, count, rows, cols), jnp.bfloat16), pltpu.SemaphoreType.DMA((2, count))]
    if last:
        in_specs.append(HBM)
        args.append(in_hbm(tables))
        out_specs = [VMEM] * 2
        out_shape = [pltpu.VMEM((tokens, cols), jnp.bfloat16)] * 2
        scratch.insert(1, pltpu.VMEM(acc_shape, jnp.float32))
        scratch.insert(2, pltpu.VMEM(tables.shape, jnp.float32))
        scratch.append(pltpu.SemaphoreType.DMA)
    else:
        out_specs = VMEM
        out_shape = pltpu.VMEM(acc_shape, jnp.float32)
    return pl.pallas_call(
        functools.partial(project_kernel, tuple(masks), first, last),
        in_specs=in_specs,
        out_specs=out_specs,
        out_shape=out_shape,
        scratch_shapes=scratch,
        compiler_params=params(10),
        cost_estimate=COST,
        name="project",
    )(*args)


HEADS = 2


def stacked(ref, r, first, count):
    rows = slice(r * TILE, (r + 1) * TILE)
    return jnp.concatenate([ref[rows, g * HD : (g + 1) * HD] for g in range(first, first + count)], axis=0)


def live_readout(ref, r, first, count, length):
    x = stacked(ref, r, first, count).astype(jnp.float32)
    at = lax.broadcasted_iota(jnp.int32, x.shape, 0) % TILE + r * TILE
    return jnp.where(at < length, x, 0.0).astype(jnp.bfloat16)


def attend_kernel(keep, len_ref, q_ref, k_ref, v_ref, ro_ref, *rest):
    groups = q_ref.shape[1] // HD
    count = min(groups, HEADS)
    seq = pl.program_id(0)
    length = len_ref[seq]
    if keep:
        before_ref, margin_ref, prob_ref, delta_ref = rest
    else:
        (margin_ref,) = rest
    score = jnp.zeros((1, count * TILE), jnp.float32)
    j = lax.broadcasted_iota(jnp.int32, (TILE, count * TILE), 0)
    i = lax.broadcasted_iota(jnp.int32, (TILE, count * TILE), 1) % TILE
    base = 0
    for r in range(LEN // TILE):
        n = (r + 1) * TILE
        for g in range(0, groups, count):
            q = stacked(q_ref, r, g, count)
            ro = live_readout(ro_ref, r, g, count, length)
            s = dot(k_ref[0:n, :], q, NT)
            dp = dot(v_ref[0:n, :], ro, NT)
            s = [s[b * TILE : (b + 1) * TILE] for b in range(r + 1)]
            s[r] = jnp.where(j <= i, s[r], -1e30)
            top = functools.reduce(jnp.maximum, [jnp.max(x, axis=0, keepdims=True) for x in s])
            e = [jnp.exp2((x - top) * (logit_scale * math.log2(math.e))) for x in s]
            inverse = 1.0 / functools.reduce(jnp.add, [jnp.sum(x, axis=0, keepdims=True) for x in e])
            cols = slice(g * TILE, (g + count) * TILE)
            delta = jnp.zeros((1, count * TILE), jnp.float32)
            for b in range(r + 1):
                p = (e[b] * inverse).astype(jnp.bfloat16)
                if keep:
                    prob_ref[0, 0, base + b * TILE : base + (b + 1) * TILE, cols] = p
                delta = delta + jnp.sum(p.astype(jnp.float32) * dp[b * TILE : (b + 1) * TILE], axis=0, keepdims=True)
            if keep:
                delta_ref[0, 0, r : r + 1, cols] = delta
            score = score + delta
        base += n
    side = jnp.where(seq % 2 == 0, 1.0, -1.0) * (dpo_beta / math.sqrt(QH * HD))

    @pl.when((seq == 0) & (pl.program_id(1) == 0))
    def _():
        margin_ref[...] = -before_ref[...] if keep else jnp.zeros_like(margin_ref)

    margin_ref[...] += jnp.broadcast_to(jnp.sum(score, axis=1, keepdims=True) * side, margin_ref.shape)


def attend(lengths, queries, keys, values, readout, before=None):
    seqs = lengths.shape[0]
    heads = keys.shape[1] // HD
    wide = queries.shape[1] // heads
    tiles = LEN // TILE
    span = TILE * tiles * (tiles + 1) // 2
    keep = before is not None
    at = lambda s, k, lens: (s, k)
    at4 = lambda s, k, lens: (s, k, 0, 0)
    fixed = lambda s, k, lens: (0, 0)
    in_specs = [pl.BlockSpec((LEN, wide), at), pl.BlockSpec((LEN, HD), at), pl.BlockSpec((LEN, HD), at), pl.BlockSpec((LEN, wide), at)]
    args = [queries, resident(keys), resident(values), readout]
    out_specs = [pl.BlockSpec((8, 128), fixed)]
    out_shape = [jax.ShapeDtypeStruct((8, 128), jnp.float32)]
    if keep:
        in_specs.append(pl.BlockSpec((8, 128), fixed))
        args.append(before)
        out_specs += [pl.BlockSpec((1, 1, span, wide), at4), pl.BlockSpec((1, 1, tiles, wide), at4)]
        out_shape += [pltpu.VMEM((seqs, heads, span, wide), jnp.bfloat16), pltpu.VMEM((seqs, heads, tiles, wide), jnp.float32)]
    return pl.pallas_call(
        functools.partial(attend_kernel, keep),
        grid_spec=pltpu.PrefetchScalarGridSpec(num_scalar_prefetch=1, grid=(seqs, heads), in_specs=in_specs, out_specs=out_specs),
        out_shape=out_shape,
        compiler_params=params(8),
        cost_estimate=COST,
        name="attend",
    )(lengths, *args)


def attend_back_kernel(len_ref, q_ref, v_ref, ro_ref, prob_ref, delta_ref, table_ref, grad_ref):
    groups = q_ref.shape[1] // HD
    count = min(groups, HEADS)
    seq = pl.program_id(0)
    length = len_ref[seq]
    tiles = LEN // TILE
    dk = [None] * tiles
    dv = [None] * tiles
    base = 0
    for r in range(tiles):
        n = (r + 1) * TILE
        for g in range(0, groups, count):
            q = stacked(q_ref, r, g, count)
            ro = live_readout(ro_ref, r, g, count, length)
            cols = slice(g * TILE, (g + count) * TILE)
            p = prob_ref[0, 0, base : base + n, cols]
            dp = dot(v_ref[0:n, :], ro, NT)
            ds = (p.astype(jnp.float32) * (dp - delta_ref[0, 0, r : r + 1, cols])).astype(jnp.bfloat16)
            tk = dot(ds, q, NN)
            tv = dot(p, ro, NN)
            for b in range(r + 1):
                at = slice(b * TILE, (b + 1) * TILE)
                dk[b] = tk[at] if dk[b] is None else dk[b] + tk[at]
                dv[b] = tv[at] if dv[b] is None else dv[b] + tv[at]
        base += n
    scale = jnp.where(seq % 2 == 0, -1.0, 1.0) * (1.0 / math.sqrt(QH * HD))
    for b in range(tiles):
        at = slice(b * TILE, (b + 1) * TILE)
        k = dk[b] * (scale * logit_scale)
        k = k * table_ref[0, at, :] - pltpu.roll(k, HD // 2, 1) * table_ref[1, at, :]
        grad_ref[0, :, at] = k.T.astype(jnp.bfloat16)
        grad_ref[1, :, at] = (dv[b] * scale).T.astype(jnp.bfloat16)


def attend_back(lengths, queries, values, readout, probs, delta, tables):
    seqs, heads, span, wide = probs.shape
    at = lambda s, k, lens: (s, k)
    at4 = lambda s, k, lens: (s, k, 0, 0)
    return pl.pallas_call(
        attend_back_kernel,
        grid_spec=pltpu.PrefetchScalarGridSpec(
            num_scalar_prefetch=1,
            grid=(seqs, heads),
            in_specs=[
                pl.BlockSpec((LEN, wide), at),
                pl.BlockSpec((LEN, HD), at),
                pl.BlockSpec((LEN, wide), at),
                pl.BlockSpec((1, 1, span, wide), at4),
                pl.BlockSpec((1, 1) + delta.shape[2:], at4),
                pl.BlockSpec(tables.shape, lambda s, k, lens: (0, 0, 0)),
            ],
            out_specs=pl.BlockSpec((2, HD, LEN), lambda s, k, lens: (0, k, s)),
        ),
        out_shape=pltpu.VMEM((2,) + values.shape[::-1], jnp.bfloat16),
        compiler_params=params(10),
        cost_estimate=COST,
        name="attend_back",
    )(lengths, queries, resident(values), readout, resident(probs), resident(delta), tables)


def gradient_tiles(idx, mask, x_ref, cot_ref, rows):
    cols = cot_ref.shape[1]
    both = jnp.concatenate([cot_ref[0], cot_ref[1]], axis=0)
    tile = min(rows, 256)
    for t in range(rows // tile):
        col = pl.multiple_of((idx ^ mask) * rows + t * tile, tile)
        out = dot(both, x_ref[:, pl.ds(col, tile)], NN)
        for i in (0, 1):
            yield i, slice(t * tile, (t + 1) * tile), out[i * cols : (i + 1) * cols]


def gradient_kernel(masks, idx_ref, x_ref, cot_ref, *outs):
    for mask, out_ref in zip(masks, outs):
        for i, at, value in gradient_tiles(idx_ref[0], mask, x_ref, cot_ref, out_ref.shape[2]):
            out_ref[i, :, at] = value.astype(out_ref.dtype)


def merged_kernel(masks, idx_ref, x_ref, cot_ref, mine_margin, their_margin, *refs):
    count = len(masks)
    theirs_hbm, outs = refs[:count], refs[count : 3 * count]
    theirs, sem = refs[3 * count :]
    copies = [pltpu.make_async_copy(theirs_hbm[n], theirs.at[n], sem.at[n]) for n in range(count)]
    for copy in copies:
        copy.start()
    weight = lambda ref: jnp.concatenate([jax.nn.sigmoid(-ref[0:1, :])] * 2, axis=1)
    mine, their = weight(mine_margin), weight(their_margin)
    for n, mask in enumerate(masks):
        copies[n].wait()
        for i, at, value in gradient_tiles(idx_ref[0], mask, x_ref, cot_ref, theirs.shape[3]):
            value = value * mine + theirs[n, i, :, at].astype(jnp.float32) * their
            outs[2 * n + i][:, at] = value.astype(outs[2 * n + i].dtype)


def gradient_blocks(idx, normed, cot, masks, rows, merge=None):
    _, cols, tokens = cot.shape
    args = [idx, resident(normed), resident(cot)]
    in_specs = [SMEM, VMEM, VMEM]
    scratch = []
    if merge is None:
        kernel, name = gradient_kernel, "gradient_block"
        out_shape = [jax.ShapeDtypeStruct((2, cols, rows), jnp.bfloat16) for m in masks]
    else:
        kernel, name = merged_kernel, "merged_block"
        margins, theirs = merge
        args += [*margins] + [theirs[m] for m in masks]
        in_specs += [VMEM, VMEM] + [HBM] * len(masks)
        out_shape = [
            jax.ShapeDtypeStruct((cols, rows), jnp.bfloat16) if m else pltpu.VMEM((cols, rows), jnp.float32)
            for m in masks
            for i in (0, 1)
        ]
        scratch = [pltpu.VMEM((len(masks), 2, cols, rows), jnp.bfloat16), pltpu.SemaphoreType.DMA((len(masks),))]
    outs = pl.pallas_call(
        functools.partial(kernel, tuple(masks)),
        in_specs=in_specs,
        out_specs=[VMEM] * len(out_shape),
        out_shape=out_shape,
        scratch_shapes=scratch,
        compiler_params=params(10),
        cost_estimate=COST,
        name=name,
    )(*args)
    return outs if merge is None else [outs[2 * n : 2 * n + 2] for n in range(len(masks))]


def finish_kernel(counts, *refs):
    refs = list(refs)
    out_ref, square_ref = refs[-2:]
    refs = refs[:-2]
    square_ref[...] = jnp.zeros_like(square_ref)
    cols, rows = refs[0].shape
    for i in (0, 1):
        terms = [refs.pop(0) for _ in range(1 + counts[i])]
        squares = jnp.zeros((1, 128), jnp.float32)
        for c in range(cols // 128):
            for r in range(rows // 128):
                at = (slice(c * 128, (c + 1) * 128), slice(r * 128, (r + 1) * 128))
                value = functools.reduce(jnp.add, [t[at].astype(jnp.float32) for t in terms])
                squares = squares + jnp.sum(value * value, axis=0, keepdims=True)
                out_ref[i, at[1], at[0]] = value.T.astype(jnp.bfloat16)
        square_ref[i : i + 1, :] = jnp.broadcast_to(jnp.sum(squares, axis=1, keepdims=True), (1, 128))


def finish(base, arrived):
    args = [x for i in (0, 1) for x in (resident(base[i]), *arrived[i])]
    cols, rows = base[0].shape
    return pl.pallas_call(
        functools.partial(finish_kernel, [len(a) for a in arrived]),
        in_specs=[VMEM] * len(args),
        out_specs=[VMEM] * 2,
        out_shape=[jax.ShapeDtypeStruct((2, rows, cols), jnp.bfloat16), jax.ShapeDtypeStruct((8, 128), jnp.float32)],
        compiler_params=params(8),
        cost_estimate=COST,
        name="finish",
    )(*args)


def fetch_kernel(masks, idx_ref, *refs):
    count = len(masks)
    pieces, (ref_hbm, w, r, sem) = refs[: 2 * count], refs[2 * count :]
    rows = r.shape[2]
    copies = []
    for n, mask in enumerate(masks):
        at = pl.ds(pl.multiple_of((idx_ref[0] ^ mask) * rows, rows), rows)
        copies += [pltpu.make_async_copy(pieces[2 * n + i], w.at[n, i], sem.at[i, n]) for i in (0, 1)]
        copies.append(pltpu.make_async_copy(ref_hbm.at[:, at, :], r.at[n], sem.at[2, n]))
    for copy in copies:
        copy.start()
    for copy in copies:
        copy.wait()


def fetch(idx, weights, reference, masks):
    rows, cols = weights[masks[0]][0].shape
    count = len(masks)
    return pl.pallas_call(
        functools.partial(fetch_kernel, tuple(masks)),
        in_specs=[SMEM] + [HBM] * (2 * count + 1),
        out_specs=[VMEM] * 2,
        out_shape=[pltpu.VMEM((count, 2, rows, cols), jnp.bfloat16)] * 2,
        scratch_shapes=[pltpu.SemaphoreType.DMA((3, count))],
        compiler_params=params(4),
        cost_estimate=COST,
        name="fetch",
    )(idx, *[w for m in masks for w in weights[m]], in_hbm(reference))


def blend_kernel(masks, first, ready, idx_ref, square_ref, *refs):
    refs = list(refs)
    count = len(masks)
    grads = [[refs.pop(0)] if whole else [refs.pop(0), refs.pop(0)] for whole in first_parts(masks, ready)]
    if ready is None:
        weights = [[refs.pop(0), refs.pop(0)] for m in masks]
        ref_hbm = refs.pop(0)
    else:
        w, r = refs.pop(0), refs.pop(0)
    if not first:
        refs.pop(0)
    out_hbm, token_ref = refs.pop(0), refs.pop(0)
    new_hbm = refs.pop(0) if first else None
    if ready is None:
        w, r = refs.pop(0), refs.pop(0)
    g, o, new, sem, out_sem = refs
    rows, cols = g.shape[2:]
    step = 32
    token_ref[...] = jnp.zeros_like(token_ref)
    copies, at = [], []
    for n in range(count):
        at.append(pl.ds(pl.multiple_of((idx_ref[0] ^ masks[n]) * rows, rows), rows))
        if len(grads[n]) == 1:
            group = [pltpu.make_async_copy(grads[n][0], g.at[n], sem.at[0, n])]
        else:
            group = [pltpu.make_async_copy(grads[n][i], g.at[n, i], sem.at[i, n]) for i in (0, 1)]
        if ready is None:
            group += [pltpu.make_async_copy(weights[n][i], w.at[n, i], sem.at[2 + i, n]) for i in (0, 1)]
            group.append(pltpu.make_async_copy(ref_hbm.at[:, at[n], :], r.at[n], sem.at[4, n]))
        for copy in group:
            copy.start()
        copies.append(group)
    mean = square_ref[...] * (1.0 / (D * KVH * HD))
    scale = jnp.concatenate([learning_rate * lax.rsqrt(mean + norm_eps)] * (cols // 128), axis=1)
    writes = []
    half = rows // 2
    for n in range(count):
        from_n = n if ready is None else ready + n
        for copy in copies[n]:
            copy.wait()
        for part in range(2):
            for i in (0, 1):
                for start in range(part * half, (part + 1) * half, step):
                    j = slice(start, start + step)
                    value = w[from_n, i, j].astype(jnp.float32) - scale[i : i + 1, :] * g[n, i, j].astype(jnp.float32)
                    value = value.astype(jnp.bfloat16)
                    if first and n == 0:
                        new[i, j] = value
                    mixed = mix_alpha * value.astype(jnp.float32) + (1.0 - mix_alpha) * r[from_n, i, j].astype(jnp.float32)
                    o[n, i, j] = mixed.astype(jnp.bfloat16)
            at_part = pl.ds(pl.multiple_of((idx_ref[0] ^ masks[n]) * rows + part * half, half), half)
            copy = pltpu.make_async_copy(o.at[n, :, pl.ds(part * half, half), :], out_hbm.at[:, at_part, :], out_sem.at[part, n])
            copy.start()
            writes.append(copy)
        if first and n == 0:
            copy = pltpu.make_async_copy(new, new_hbm, out_sem.at[0, count])
            copy.start()
            writes.append(copy)
    for copy in writes:
        copy.wait()


def first_parts(masks, ready):
    return [len(bits_of(m >> 1)) < 2 for m in masks]


def blend(idx, squares, weights, grads, reference, held, masks, ready=None):
    rows, cols = weights[masks[0]][0].shape
    count = len(masks)
    first = held is None
    args = [idx, squares] + [x for m in masks for x in grads[m]]
    in_specs = [SMEM, VMEM] + [HBM] * (len(args) - 2)
    block = pltpu.VMEM((count, 2, rows, cols), jnp.bfloat16)
    scratch = [block, block, pltpu.VMEM((2, rows, cols) if first else (8, 128), jnp.bfloat16)]
    scratch += [pltpu.SemaphoreType.DMA((5, count)), pltpu.SemaphoreType.DMA((2, count + 1))]
    if ready is None:
        args += [w for m in masks for w in weights[m]] + [in_hbm(reference)]
        in_specs += [HBM] * (2 * count + 1)
        scratch = [block, block] + scratch
    else:
        args += [resident(x) for x in ready[0]]
        in_specs += [VMEM] * 2
    out_specs = [HBM, VMEM]
    out_shape = [jax.ShapeDtypeStruct(reference.shape, jnp.bfloat16), jax.ShapeDtypeStruct((8, 128), jnp.float32)]
    aliases = {}
    if first:
        out_specs.append(HBM)
        out_shape.append(jax.ShapeDtypeStruct((2, rows, cols), jnp.bfloat16))
    else:
        aliases = {len(args): 0}
        in_specs.append(HBM)
        args.append(held)
    return pl.pallas_call(
        functools.partial(blend_kernel, tuple(masks), first, None if ready is None else ready[1]),
        in_specs=in_specs,
        out_specs=out_specs,
        out_shape=out_shape,
        scratch_shapes=scratch,
        input_output_aliases=aliases,
        compiler_params=params(6 + 5 * count),
        cost_estimate=COST,
        name="blend",
    )(*args)


def bits_of(mask):
    return [1 << b for b in range(mask.bit_length()) if mask >> b & 1]


def after(value, *earlier):
    return lax.optimization_barrier((value, earlier))[0]


def body(shards, tensors, hidden_in, policy_weights, reference_weights, policy_queries, reference_queries, readout, lengths):
    rows = policy_weights.shape[1]
    idx = lax.axis_index("shard").astype(jnp.int32).reshape(1)
    tables = jnp.asarray(rope_tables())

    def swap(x, bit, axis="shard", size=shards):
        return lax.ppermute(x, axis, [(i, i ^ bit) for i in range(size)])

    def powers(size):
        return [1 << b for b in range(size.bit_length() - 1)]

    chips = sorted(range(0, shards, 2), key=lambda m: (len(bits_of(m)), m))
    near = [m for m in chips if len(bits_of(m)) == 1]
    far = [m for m in chips if len(bits_of(m)) > 1]
    link = lambda i, m: bits_of(m)[-1] if i == 0 else bits_of(m)[0]

    def send_near(own):
        got = {0: list(own)}
        for turn in (0, 1):
            for n, m in enumerate(near):
                i = (turn + n) % 2
                got.setdefault(m, [None, None])[i] = swap(own[i], m)
        got[1] = [swap(g, 1) for g in own]
        return got

    def send_whole(own):
        got = {m: [swap(own, m)] for m in near}
        got[0] = [own]
        got[1] = [swap(own, 1)]
        return got

    def relay(got, m, *earlier):
        got[m] = [None, None]
        for i in (0, 1):
            via = link(i, m)
            source = got[m ^ via]
            source = source[i] if len(source) == 2 else source[0][i]
            got[m][i] = swap(after(source, *earlier), via)

    def to_core(got, m, *earlier):
        got[m | 1] = [swap(after(g, *earlier), 1) for g in got[m]]

    weights = send_near((policy_weights[0], policy_weights[1]))
    normed, ref_keys, ref_values = norm_project(hidden_in, reference_weights, tables)
    for m in far:
        relay(weights, m, ref_keys)
    (ref_margin,) = attend(lengths, reference_queries, ref_keys, ref_values, readout)
    for m in near:
        to_core(weights, m, ref_margin)
    early = [m | c for m in [0] + near for c in (0, 1)]
    held = project(after(idx, ref_margin), normed, early, weights, None, None if far else tables)
    if far:
        for m in far:
            to_core(weights, m, held)
        held = project(idx, normed, [m | c for m in far for c in (0, 1)], weights, held, tables)
    pol_keys, pol_values = held
    margin, probs, delta = attend(lengths, policy_queries, pol_keys, pol_values, readout, ref_margin)

    theirs = {}
    order = list(reversed(chips))
    split = max(len(far), 1)

    def backward():
        return attend_back(lengths, policy_queries, pol_values, readout, probs, delta, tables)

    def other_blocks():
        done = []
        for masks in (order[:split], order[split:]):
            blocks = gradient_blocks(after(idx, margin), normed, cot, [m | 1 for m in masks], rows)
            theirs.update({m: swap(block, 1) for m, block in zip(masks, blocks)})
            done += blocks
        return done

    cot = None
    for bit in powers(tensors):
        received = swap(margin, bit, "tensor", tensors)
        if cot is None:
            received = after(received, cot := backward())
        elif not theirs:
            received = after(received, other_blocks())
        margin = margin + received
    if cot is None:
        cot = backward()
    if not theirs:
        other_blocks()
    margins = (margin, swap(margin, 1))

    chip_sum = {}
    arrived = {m: [[], []] for m in chips}
    waiting = []

    def send(m, i):
        payload = chip_sum[m][i]
        if arrived[m][i]:
            payload = payload.astype(jnp.float32)
            for term in arrived[m][i]:
                payload = payload + term.astype(jnp.float32)
            payload = payload.astype(jnp.bfloat16)
        via = link(i, m)
        arrived[m ^ via][i].append(swap(payload, via))
        return payload

    last = margins[1]
    for masks in (order[:split], order[split:]):
        blocks = gradient_blocks(after(idx, last), normed, cot, masks, rows, (margins, theirs))
        chip_sum.update(zip(masks, blocks))
        last = blocks
        for m in masks:
            for i in (0, 1):
                if m and not any(k ^ link(i, k) == m for k in far):
                    send(m, i)
                elif m:
                    waiting.append((m, i))
    for m, i in waiting:
        arrived[m][i] = [after(term, last) for term in arrived[m][i]]
        send(m, i)
    own, squares = finish(chip_sum[0], arrived[0])

    grads = send_whole(own)
    for bit in powers(tensors):
        squares = squares + swap(squares, bit, "tensor", tensors)
    for bit in powers(shards):
        squares = squares + swap(squares, bit)
    for m in far:
        relay(grads, m, squares)
    for m in near:
        to_core(grads, m)
    new_reference, token, new_policy = blend(idx, squares, weights, grads, reference_weights, None, early)
    if far:
        ready = fetch(after(idx, token), weights, reference_weights, [m | c for c in (0, 1) for m in far])
        for m in far:
            to_core(grads, m, ready)
        for c in (0, 1):
            masks = [m | c for m in far]
            new_reference, token = blend(idx, squares, weights, grads, reference_weights, new_reference, masks, (ready, c * len(far)))
    return (new_policy, new_reference, margin[0, :1])


def solution(mesh):
    return jax.shard_map(
        functools.partial(body, mesh.shape["shard"], mesh.shape["tensor"]),
        mesh=mesh,
        in_specs=(
            P("shard", None),
            P(None, "shard", "tensor"),
            P(None, None, "tensor"),
            P("shard", "tensor"),
            P("shard", "tensor"),
            P("shard", "tensor"),
            P("shard"),
        ),
        out_specs=(P(None, "shard", "tensor"), P(None, None, "tensor"), P("shard")),
        check_vma=False,
    )
```

time: 217 us -> 179 us (0.82)
  Pallas kernels: 95.5 us -> 63.4 us
  local copies, waits for them, and re-layouts: 30.8 us -> 16.6 us
  waiting for transfers between devices: 53 us -> 64.1 us
  other arithmetic: 2.7 us -> 0.41 us
    pallas_call x17 -> x14, Pallas kernels: 94.8 us -> 62.8 us  [the longest x1 14.3 us: norm_project(): pl.pallas_call(norm_project_kernel, in_specs=[HBM, HBM, HBM], out_specs=[...]
    unnamed x62 -> x38, local copies, waits for them, and re-layouts: 26.5 us -> 14.7 us
    ppermute x46 -> x41, waiting for transfers between devices: 53 us -> 64.1 us  [swap(): return lax.ppermute(x, axis, [(i, i ^ bit) for i in range(size)])]
    ppermute x46 -> x41, starting transfers between devices: 33.1 us -> 32.6 us  [swap(): return lax.ppermute(x, axis, [(i, i ^ bit) for i in range(size)])]
  transfers between devices with their start and end apart: 46 -> 41, of which waited for: 19 -> 14; matrix products, arithmetic and copies ran while one was open for 1% -> 1% of each run, Pallas kernels for 32% -> 28%
where the time goes in v1:
time: 179 us; the launch traced here: 178 us
  waiting for transfers between devices  64.1 us (36%)
  Pallas kernels  63.4 us (35%)
  starting transfers between devices  32.6 us (18%)
  local copies, waits for them, and re-layouts  16.6 us (9%)
    ppermute x41, waiting for transfers between devices, swap(): return lax.ppermute(x, axis, [(i, i ^ bit) for i in range(size)])  64.1 us
    ppermute x41, starting transfers between devices, swap(): return lax.ppermute(x, axis, [(i, i ^ bit) for i in range(size)])  32.6 us
    unnamed x38, local copies, waits for them, and re-layouts  14.7 us
    pallas_call x1, Pallas kernels, norm_project(): pl.pallas_call(norm_project_kernel, in_specs=[HBM, HBM, HBM], out_specs=[...  14.3 us
    pallas_call x3, Pallas kernels, blend(): pl.pallas_call(functools.partial(blend_kernel, tuple(masks), first, None...  12.8 us
    pallas_call x2, Pallas kernels, attend(): pl.pallas_call(functools.partial(attend_kernel, keep), grid_spec=pltpu.Pr...  9.64 us
    pallas_call x2, Pallas kernels, project(): pl.pallas_call(functools.partial(project_kernel, tuple(masks), first, las...  9.38 us
    pallas_call x4, Pallas kernels, gradient_blocks(): pl.pallas_call(functools.partial(kernel, tuple(masks)), in_specs=in_specs...  8.09 us
  transfers between devices with their start and end apart: 41, of which 14 were waited for; matrix products, arithmetic and copies ran while one was open for 1% of the time, Pallas kernels for 28%

profile of v1, /device:TPU:0, one launch (start us, length us, event | category | flops | bytes accessed | tf_op | source)
XLA Modules:
  0.0 178.3 jit_solution(17583240917548615092)
XLA Ops:
  0.6 1.3 slice_bitcast_fusion.2
  1.9 3.0 %collective-permute-start.9 = (bf16[1024,256]{1,0:T(8,128)(2,1)S(1)}, bf16[1024,256]{1,0:T(8,128)(2,1)S(1)}, u32[]{:S(2)}, u32[]{:S(2)}) collective-permute-start(bf16[1024,256]{1,0:T(8,128)(2,1)S(1)} %get-tuple-element.97.refs_6_.refs_7_), channel_id=1, source_target_pairs={{0,16},{4,20},{8,24},{12,28},{16,0},{20,4},{24,8},{28,12},{1,17},{... | collective-permute-start | bytes 1572872 | tf_op jit(solution)/shard_map/ppermute | solution.py:616
  4.9 1.5 collective-permute-start
  6.4 0.5 collective-permute-start.4
  7.1 14.3 %norm_project.1 = (bf16[768,8192]{1,0:T(8,128)(2,1)S(1)}, bf16[768,256]{1,0:T(8,128)(2,1)S(1)}, bf16[768,256]{1,0:T(8,128)(2,1)S(1)}) custom-call(bf16[768,8192]{1,0:T(8,128)(2,1)} %hidden_hbm.1, bf16[2,8192,256]{2,1,0:T(8,128)(2,1)} %refs_4_.1, f32[2,384,128]{2,1,0:T(8,128)} %constant.8.clone.table_hbm.refs_5_.table_ref), custom_call_target="tpu_custom_call" | custom-call | flops 1 | bytes 1 | tf_op jit(solution)/shard_map/norm_project/pallas_call | solution.py:127
  21.4 4.6 %copy-done = bf16[768,8192]{1,0:T(8,128)(2,1)} copy-done((bf16[768,8192]{1,0:T(8,128)(2,1)}, bf16[768,8192]{1,0:T(8,128)(2,1)S(1)}, u32[]{:S(2)}) %copy-start) | copy-done | bytes 12582936
  26.0 4.6 %attend.2.rest_0_ = f32[8,128]{1,0:T(8,128)S(1)} custom-call(s32[2]{0:T(128)S(1)} %copy-done.15, bf16[768,1024]{1,0:T(8,128)(2,1)S(1)} %copy-done.14, bf16[768,256]{1,0:T(8,128)(2,1)S(1)} %get-tuple-element.51.k_ref, bf16[768,256]{1,0:T(8,128)(2,1)S(1)} %get-tuple-element.53.v_ref, bf16[768,1024]{1,0:T(8,128)(2,1)S(1)} %copy-done.2), custom_call_target="tpu_custom_call" | custom-call | flops 1 | bytes 1 | tf_op jit(solution)/shard_map/attend/pallas_call | solution.py:300
  30.6 0.5 collective-permute-start.6
  31.8 0.8 copy-done.5
  33.0 0.8 copy-done.8
  33.8 1.9 %collective-permute-start.12 = (bf16[1024,256]{1,0:T(8,128)(2,1)S(1)}, bf16[1024,256]{1,0:T(8,128)(2,1)}, u32[]{:S(2)}, u32[]{:S(2)}) collective-permute-start(bf16[1024,256]{1,0:T(8,128)(2,1)S(1)} %collective-permute-done.9.refs_10_.refs_15_), channel_id=1, source_target_pairs={{0,8},{4,12},{8,0},{12,4},{16,24},{20,28},{24,16},{28,20},{1,9},{5... | collective-permute-start | bytes 1572872 | tf_op jit(solution)/shard_map/ppermute | solution.py:616
  35.7 0.8 copy-done.11
  36.5 1.5 collective-permute-start.1
  38.0 4.6 %copy-done.1 = bf16[768,8192]{1,0:T(8,128)(2,1)S(1)} copy-done((bf16[768,8192]{1,0:T(8,128)(2,1)S(1)}, bf16[768,8192]{1,0:T(8,128)(2,1)}, u32[]{:S(2)}) %copy-start.1) | copy-done | bytes 12582936
  42.6 1.0 copy-done.6
  43.7 1.0 copy-done.9
  44.7 1.0 copy-done.12
  45.7 5.6 %project.2.refs_4_ = f32[2,768,256]{2,1,0:T(8,128)S(1)} custom-call(s32[1]{0:T(128)} %bitcast.idx_ref, bf16[768,8192]{1,0:T(8,128)(2,1)S(1)} %copy-done.1, bf16[1024,256]{1,0:T(8,128)(2,1)S(1)} %get-tuple-element.98.refs_0_.refs_6_, bf16[1024,256]{1,0:T(8,128)(2,1)S(1)} %copy-done.6, bf16[1024,256]{1,0:T(8,128)(2,1)} %collective-permute-done.refs_2_.refs_10_, ...), custom_call_target="tpu_custom_call" | custom-call | flops 1 | bytes 1 | tf_op jit(solution)/shard_map/project/pallas_call | solution.py:210
  51.5 0.5 collective-permute-start.11
  52.0 1.6 collective-permute-done.13.refs_3_
  53.6 0.7 collective-permute-done.11.refs_1_.refs_2_
  54.3 3.8 %project.3 = (bf16[768,256]{1,0:T(8,128)(2,1)S(1)}, bf16[768,256]{1,0:T(8,128)(2,1)S(1)}) custom-call(s32[1]{0:T(128)} %bitcast.idx_ref, bf16[768,8192]{1,0:T(8,128)(2,1)S(1)} %copy-done.1, bf16[1024,256]{1,0:T(8,128)(2,1)} %collective-permute-done.1.refs_0_, bf16[1024,256]{1,0:T(8,128)(2,1)S(1)} %collective-permute-done.11.refs_1_.refs_2_, ...), custom_call_target="tpu_custom_call" | custom-call | flops 1 | bytes 1 | tf_op jit(solution)/shard_map/project/pallas_call | solution.py:210
  58.1 5.0 %attend.3 = (f32[8,128]{1,0:T(8,128)S(1)}, bf16[2,2,768,512]{3,2,1,0:T(8,128)(2,1)S(1)}, f32[2,2,3,512]{3,2,1,0:T(4,128)S(1)}) custom-call(s32[2]{0:T(128)S(1)} %copy-done.15, bf16[768,1024]{1,0:T(8,128)(2,1)S(1)} %copy-done.3, bf16[768,256]{1,0:T(8,128)(2,1)S(1)} %get-tuple-element.62.k_ref, bf16[768,256]{1,0:T(8,128)(2,1)S(1)} %get-tuple-element.63.v_ref, ...), custom_call_target="tpu_custom_call" | custom-call | flops 1 | bytes 1 | tf_op jit(solution)/shard_map/attend/pallas_call | solution.py:300
  63.1 1.6 collective-permute-start.14
  64.7 6.6 %attend_back.1.cot_ref = bf16[2,256,768]{2,1,0:T(8,128)(2,1)S(1)} custom-call(s32[2]{0:T(128)S(1)} %copy-done.15, bf16[768,1024]{1,0:T(8,128)(2,1)S(1)} %copy-done.3, bf16[768,256]{1,0:T(8,128)(2,1)S(1)} %get-tuple-element.63.v_ref, bf16[768,1024]{1,0:T(8,128)(2,1)S(1)} %copy-done.2, bf16[2,2,768,512]{3,2,1,0:T(8,128)(2,1)S(1)} %get-tuple-element.65.prob_ref, ...), custom_call_target="tpu_custom_call" | custom-call | flops 1 | bytes 1 | tf_op jit(solution)/shard_map/attend_back/pallas_call | solution.py:348
  71.4 1.0 gradient_block.2
  72.5 2.7 %gradient_block.3 = (bf16[2,256,1024]{2,1,0:T(8,128)(2,1)S(1)}, bf16[2,256,1024]{2,1,0:T(8,128)(2,1)S(1)}, bf16[2,256,1024]{2,1,0:T(8,128)(2,1)S(1)}) custom-call(s32[1]{0:T(128)} %bitcast.idx_ref, bf16[768,8192]{1,0:T(8,128)(2,1)S(1)} %bitcast.11, bf16[2,256,768]{2,1,0:T(8,128)(2,1)S(1)} %attend_back.1.cot_ref), custom_call_target="tpu_custom_call" | custom-call | flops 1 | bytes 1 | tf_op jit(solution)/shard_map/gradient_block/pallas_call | solution.py:422
  75.2 0.6 collective-permute-start.18
  76.2 2.6 %collective-permute-start.15 = (f32[8,128]{1,0:T(8,128)S(1)}, f32[8,128]{1,0:T(8,128)S(1)}, u32[]{:S(2)}, u32[]{:S(2)}) collective-permute-start(f32[8,128]{1,0:T(8,128)S(1)} %add.27), channel_id=1, source_target_pairs={{0,2},{1,3},{2,0},{3,1},{4,6},{5,7},{6,4},{7,5},{8,10},{9,11},{10,... | collective-permute-start | bytes 12296 | tf_op jit(solution)/shard_map/ppermute | solution.py:616
  78.8 1.9 %collective-permute-done.15 = f32[8,128]{1,0:T(8,128)S(1)} collective-permute-done((f32[8,128]{1,0:T(8,128)S(1)}, f32[8,128]{1,0:T(8,128)S(1)}, u32[]{:S(2)}, u32[]{:S(2)}) %collective-permute-start.15) | collective-permute-done | bytes 4128 | tf_op jit(solution)/shard_map/ppermute | solution.py:616
  80.7 1.2 collective-permute-done.16.their_margin
  81.9 1.1 merged_block.2
  83.0 0.6 collective-permute-start.25
  83.6 0.9 collective-permute-start.22
  84.5 3.3 %merged_block.3 = (bf16[256,1024]{1,0:T(8,128)(2,1)S(1)}, bf16[256,1024]{1,0:T(8,128)(2,1)S(1)}, bf16[256,1024]{1,0:T(8,128)(2,1)S(1)}, bf16[256,1024]{1,0:T(8,1...) custom-call(s32[1]{0:T(128)} %bitcast.idx_ref, bf16[768,8192]{1,0:T(8,128)(2,1)S(1)} %bitcast.11, ...), custom_call_target="tpu_custom_call" | custom-call | flops 1 | bytes 1 | tf_op jit(solution)/shard_map/merged_block/pallas_call | solution.py:422
  87.9 1.2 collective-permute-start.21
  89.0 1.5 collective-permute-start.24
  90.5 7.3 %collective-permute-done.25 = bf16[256,1024]{1,0:T(8,128)(2,1)S(1)} collective-permute-done((bf16[256,1024]{1,0:T(8,128)(2,1)S(1)}, bf16[256,1024]{1,0:T(8,128)(2,1)S(1)}, u32[]{:S(2)}, u32[]{:S(2)}) %collective-permute-start.25) | collective-permute-done | bytes 524320 | tf_op jit(solution)/shard_map/ppermute | solution.py:616
  98.0 0.6 collective-permute-start.26
  98.8 1.4 collective-permute-start.23
  100.2 9.5 %collective-permute-done.21.refs_1_ = bf16[256,1024]{1,0:T(8,128)(2,1)S(1)} collective-permute-done((bf16[256,1024]{1,0:T(8,128)(2,1)S(1)}, bf16[256,1024]{1,0:T(8,128)(2,1)S(1)}, u32[]{:S(2)}, u32[]{:S(2)}) %collective-permute-start.21) | collective-permute-done | bytes 524320 | tf_op jit(solution)/shard_map/ppermute | solution.py:616
  109.7 10.1 %collective-permute-done.26.refs_5_ = bf16[256,1024]{1,0:T(8,128)(2,1)S(1)} collective-permute-done((bf16[256,1024]{1,0:T(8,128)(2,1)S(1)}, bf16[256,1024]{1,0:T(8,128)(2,1)S(1)}, u32[]{:S(2)}, u32[]{:S(2)}) %collective-permute-start.26) | collective-permute-done | bytes 524320 | tf_op jit(solution)/shard_map/ppermute | solution.py:616
  119.8 0.7 finish.1
  120.5 1.0 collective-permute-start.35
  121.5 1.1 collective-permute-start.33
  122.5 0.4 collective-permute-start.27
  123.0 3.2 %collective-permute-done.27 = f32[8,128]{1,0:T(8,128)S(1)} collective-permute-done((f32[8,128]{1,0:T(8,128)S(1)}, f32[8,128]{1,0:T(8,128)S(1)}, u32[]{:S(2)}, u32[]{:S(2)}) %collective-permute-start.27) | collective-permute-done | bytes 4128 | tf_op jit(solution)/shard_map/ppermute | solution.py:616
  126.1 2.6 %collective-permute-start.28 = (f32[8,128]{1,0:T(8,128)S(1)}, f32[8,128]{1,0:T(8,128)S(1)}, u32[]{:S(2)}, u32[]{:S(2)}) collective-permute-start(f32[8,128]{1,0:T(8,128)S(1)} %add.31), channel_id=1, source_target_pairs={{0,2},{1,3},{2,0},{3,1},{4,6},{5,7},{6,4},{7,5},{8,10},{9,11},{10,... | collective-permute-start | bytes 12296 | tf_op jit(solution)/shard_map/ppermute | solution.py:616
  128.7 1.9 %collective-permute-done.28 = f32[8,128]{1,0:T(8,128)S(1)} collective-permute-done((f32[8,128]{1,0:T(8,128)S(1)}, f32[8,128]{1,0:T(8,128)S(1)}, u32[]{:S(2)}, u32[]{:S(2)}) %collective-permute-start.28) | collective-permute-done | bytes 4128 | tf_op jit(solution)/shard_map/ppermute | solution.py:616
  130.7 1.2 collective-permute-done.29
  131.8 0.9 collective-permute-start.30
  132.8 12.6 %collective-permute-done.30 = f32[8,128]{1,0:T(8,128)S(1)} collective-permute-done((f32[8,128]{1,0:T(8,128)S(1)}, f32[8,128]{1,0:T(8,128)S(1)}, u32[]{:S(2)}, u32[]{:S(2)}) %collective-permute-start.30) | collective-permute-done | bytes 4128 | tf_op jit(solution)/shard_map/ppermute | solution.py:616
  145.3 1.2 collective-permute-start.31
  146.5 2.4 %collective-permute-done.31 = f32[8,128]{1,0:T(8,128)S(1)} collective-permute-done((f32[8,128]{1,0:T(8,128)S(1)}, f32[8,128]{1,0:T(8,128)S(1)}, u32[]{:S(2)}, u32[]{:S(2)}) %collective-permute-start.31) | collective-permute-done | bytes 4128 | tf_op jit(solution)/shard_map/ppermute | solution.py:616
  149.0 1.1 collective-permute-start.39
  150.3 0.5 collective-permute-start.36
  150.8 1.5 collective-permute-start.37
  152.3 1.9 %fetch.1 = (bf16[2,2,1024,256]{3,2,1,0:T(8,128)(2,1)S(1)}, bf16[2,2,1024,256]{3,2,1,0:T(8,128)(2,1)S(1)}) custom-call(s32[1]{0:T(128)} %bitcast.idx_ref, bf16[1024,256]{1,0:T(8,128)(2,1)} %collective-permute-done.1.refs_0_, bf16[1024,256]{1,0:T(8,128)(2,1)} %collective-permute-done.12.refs_2_.refs_1_, ...), custom_call_target="tpu_custom_call" | custom-call | flops 1 | bytes 1 | tf_op jit(solution)/shard_map/fetch/pallas_call | solution.py:485
  154.3 6.7 %collective-permute-done.39.refs_1_ = bf16[1024,256]{1,0:T(8,128)(2,1)S(1)} collective-permute-done((bf16[1024,256]{1,0:T(8,128)(2,1)S(1)}, bf16[1024,256]{1,0:T(8,128)(2,1)S(1)}, u32[]{:S(2)}, u32[]{:S(2)}) %collective-permute-start.39) | collective-permute-done | bytes 524320 | tf_op jit(solution)/shard_map/ppermute | solution.py:616
  161.0 3.7 %collective-permute-done.37.refs_0_ = bf16[1024,256]{1,0:T(8,128)(2,1)S(1)} collective-permute-done((bf16[1024,256]{1,0:T(8,128)(2,1)S(1)}, bf16[1024,256]{1,0:T(8,128)(2,1)S(1)}, u32[]{:S(2)}, u32[]{:S(2)}) %collective-permute-start.37) | collective-permute-done | bytes 524320 | tf_op jit(solution)/shard_map/ppermute | solution.py:616
  164.7 0.5 slice.19
  165.3 8.4 %blend.3 = (bf16[2,8192,256]{2,1,0:T(8,128)(2,1)}, f32[8,128]{1,0:T(8,128)}, bf16[2,1024,256]{2,1,0:T(8,128)(2,1)}) custom-call(s32[1]{0:T(128)} %bitcast.idx_ref, f32[8,128]{1,0:T(8,128)S(1)} %add.35.square_ref, bf16[2,1024,256]{2,1,0:T(8,128)(2,1)S(1)} %get-tuple-element.86.refs_0_, bf16[2,1024,256]{2,1,0:T(8,128)(2,1)S(1)} %collective-permute-done.32.refs_1_, ...), custom_call_target="tpu_custom_call" | custom-call | flops 1 | bytes 1 | tf_op jit(solution)/shard_map/blend/pallas_call | solution.py:589
  173.6 2.2 %blend.4 = (bf16[2,8192,256]{2,1,0:T(8,128)(2,1)}, f32[8,128]{1,0:T(8,128)}) custom-call(s32[1]{0:T(128)} %bitcast.idx_ref, f32[8,128]{1,0:T(8,128)S(1)} %add.35.square_ref, bf16[1024,256]{1,0:T(8,128)(2,1)S(1)} %collective-permute-done.37.refs_0_, bf16[1024,256]{1,0:T(8,128)(2,1)S(1)} %collective-permute-done.39.refs_1_, ...), custom_call_target="tpu_custom_call", output_to_operand_aliasing={{0}: (6, {})} | custom-call | flops 1 | bytes 1 | tf_op jit(solution)/shard_map/blend/pallas_call | solution.py:589
  175.9 2.2 %blend.5 = (bf16[2,8192,256]{2,1,0:T(8,128)(2,1)}, f32[8,128]{1,0:T(8,128)}) custom-call(s32[1]{0:T(128)} %bitcast.idx_ref, f32[8,128]{1,0:T(8,128)S(1)} %add.35.square_ref, bf16[1024,256]{1,0:T(8,128)(2,1)S(1)} %collective-permute-done.38.refs_0_, bf16[1024,256]{1,0:T(8,128)(2,1)S(1)} %collective-permute-done.40.refs_1_, ...), custom_call_target="tpu_custom_call", output_to_operand_aliasing={{0}: (6, {})} | custom-call | flops 1 | bytes 1 | tf_op jit(solution)/shard_map/blend/pallas_call | solution.py:589
  (85 shorter events, 2.5 us)
Async XLA Ops:
  1.9 28.7 %collective-permute-start.9 = (bf16[1024,256]{1,0:T(8,128)(2,1)S(1)}, bf16[1024,256]{1,0:T(8,128)(2,1)S(1)}, u32[]{:S(2)}, u32[]{:S(2)}) collective-permute-start(bf16[1024,256]{1,0:T(8,128)(2,1)S(1)} %get-tuple-element.97.refs_6_.refs_7_), channel_id=1, source_target_pairs={{0,16},{4,20},{8,24},{12,28},{16,0},{20,4},{24,8},{28,12},{1,17},{... | collective-permute-start | bytes 1572872 | tf_op jit(solution)/shard_map/ppermute | solution.py:616
  4.9 21.1 %copy-start.2 = (bf16[768,1024]{1,0:T(8,128)(2,1)S(1)}, bf16[768,1024]{1,0:T(8,128)(2,1)}, u32[]{:S(2)}) copy-start(bf16[768,1024]{1,0:T(8,128)(2,1)} %ro_ref.5) | copy-start | bytes 4718596
  4.9 21.1 %copy-start.14 = (bf16[768,1024]{1,0:T(8,128)(2,1)S(1)}, bf16[768,1024]{1,0:T(8,128)(2,1)}, u32[]{:S(2)}) copy-start(bf16[768,1024]{1,0:T(8,128)(2,1)} %q_ref.3) | copy-start | bytes 4718596
  4.9 21.1 %copy-start.15 = (s32[2]{0:T(128)S(1)}, s32[2]{0:T(128)}, u32[]{:S(2)}) copy-start(s32[2]{0:T(128)} %len_ref.5) | copy-start | bytes 28
  4.9 26.2 %collective-permute-start = (bf16[1024,256]{1,0:T(8,128)(2,1)S(1)}, bf16[1024,256]{1,0:T(8,128)(2,1)}, u32[]{:S(2)}, u32[]{:S(2)}) collective-permute-start(bf16[1024,256]{1,0:T(8,128)(2,1)S(1)} %get-tuple-element.98.refs_0_.refs_6_), channel_id=1, source_target_pairs={{0,8},{4,12},{8,0},{12,4},{16,24},{20,28},{24,16},{28,20},{1,9},{5... | collective-permute-start | bytes 1572872 | tf_op jit(solution)/shard_map/ppermute | solution.py:616
  6.4 24.8 %collective-permute-start.4 = (bf16[1024,256]{1,0:T(8,128)(2,1)S(1)}, bf16[1024,256]{1,0:T(8,128)(2,1)}, u32[]{:S(2)}, u32[]{:S(2)}) collective-permute-start(bf16[1024,256]{1,0:T(8,128)(2,1)S(1)} %get-tuple-element.98.refs_0_.refs_6_), channel_id=1, source_target_pairs={{0,16},{4,20},{8,24},{12,28},{16,0},{20,4},{24,8},{28,12},{1,17},{... | collective-permute-start | bytes 1572872 | tf_op jit(solution)/shard_map/ppermute | solution.py:616
  6.9 24.8 %collective-permute-start.7 = (bf16[1024,256]{1,0:T(8,128)(2,1)S(1)}, bf16[1024,256]{1,0:T(8,128)(2,1)}, u32[]{:S(2)}, u32[]{:S(2)}) collective-permute-start(bf16[1024,256]{1,0:T(8,128)(2,1)S(1)} %get-tuple-element.97.refs_6_.refs_7_), channel_id=1, source_target_pairs={{0,8},{4,12},{8,0},{12,4},{16,24},{20,28},{24,16},{28,20},{1,9},{5... | collective-permute-start | bytes 1572872 | tf_op jit(solution)/shard_map/ppermute | solution.py:616
  7.1 24.7 %collective-permute-start.2 = (bf16[1024,256]{1,0:T(8,128)(2,1)S(1)}, bf16[1024,256]{1,0:T(8,128)(2,1)S(1)}, u32[]{:S(2)}, u32[]{:S(2)}) collective-permute-start(bf16[1024,256]{1,0:T(8,128)(2,1)S(1)} %get-tuple-element.98.refs_0_.refs_6_), channel_id=1, source_target_pairs={{0,4},{4,0},{8,12},{12,8},{16,20},{20,16},{24,28},{28,24},{1,5},{5... | collective-permute-start | bytes 1572872 | tf_op jit(solution)/shard_map/ppermute | solution.py:616
  21.4 4.6 %copy-start = (bf16[768,8192]{1,0:T(8,128)(2,1)}, bf16[768,8192]{1,0:T(8,128)(2,1)S(1)}, u32[]{:S(2)}) copy-start(bf16[768,8192]{1,0:T(8,128)(2,1)S(1)} %get-tuple-element.50.x_ref) | copy-start | bytes 37748740
  30.6 2.4 %collective-permute-start.6 = (bf16[1024,256]{1,0:T(8,128)(2,1)S(1)}, bf16[1024,256]{1,0:T(8,128)(2,1)S(1)}, u32[]{:S(2)}, u32[]{:S(2)}) collective-permute-start(bf16[1024,256]{1,0:T(8,128)(2,1)S(1)} %get-tuple-element.97.refs_6_.refs_7_), channel_id=1, source_target_pairs={{0,4},{4,0},{8,12},{12,8},{16,20},{20,16},{24,28},{28,24},{1,5},{5... | collective-permute-start | bytes 1572872 | tf_op jit(solution)/shard_map/ppermute | solution.py:616
  31.2 4.5 %collective-permute-start.10 = (bf16[1024,256]{1,0:T(8,128)(2,1)S(1)}, bf16[1024,256]{1,0:T(8,128)(2,1)S(1)}, u32[]{:S(2)}, u32[]{:S(2)}) collective-permute-start(bf16[1024,256]{1,0:T(8,128)(2,1)S(1)} %collective-permute-done.9.refs_10_.refs_15_), channel_id=1, source_target_pairs={{0,4},{4,0},{8,12},{12,8},{16,20},{20,16},{24,28},{28,24},{1,5},{5... | collective-permute-start | bytes 1572872 | tf_op jit(solution)/shard_map/ppermute | solution.py:616
  31.3 6.8 %collective-permute-start.3 = (bf16[1024,256]{1,0:T(8,128)(2,1)}, bf16[1024,256]{1,0:T(8,128)(2,1)}, u32[]{:S(2)}, u32[]{:S(2)}) collective-permute-start(bf16[1024,256]{1,0:T(8,128)(2,1)} %collective-permute-done.refs_2_.refs_10_), channel_id=1, source_target_pairs={{0,4},{4,0},{8,12},{12,8},{16,20},{20,16},{24,28},{28,24},{1,5},{5... | collective-permute-start | bytes 1572872 | tf_op jit(solution)/shard_map/ppermute | solution.py:616
  31.7 6.3 %collective-permute-start.5 = (bf16[1024,256]{1,0:T(8,128)(2,1)}, bf16[1024,256]{1,0:T(8,128)(2,1)}, u32[]{:S(2)}, u32[]{:S(2)}) collective-permute-start(bf16[1024,256]{1,0:T(8,128)(2,1)} %collective-permute-done.4.refs_4_.refs_14_), channel_id=1, source_target_pairs={{0,4},{4,0},{8,12},{12,8},{16,20},{20,16},{24,28},{28,24},{1,5},{5... | collective-permute-start | bytes 1572872 | tf_op jit(solution)/shard_map/ppermute | solution.py:616
  31.8 0.8 copy-start.5
  32.6 5.4 %collective-permute-start.8 = (bf16[1024,256]{1,0:T(8,128)(2,1)}, bf16[1024,256]{1,0:T(8,128)(2,1)}, u32[]{:S(2)}, u32[]{:S(2)}) collective-permute-start(bf16[1024,256]{1,0:T(8,128)(2,1)} %collective-permute-done.7.refs_8_.refs_11_), channel_id=1, source_target_pairs={{0,4},{4,0},{8,12},{12,8},{16,20},{20,16},{24,28},{28,24},{1,5},{5... | collective-permute-start | bytes 1572872 | tf_op jit(solution)/shard_map/ppermute | solution.py:616
  33.0 0.8 copy-start.8
  33.8 17.6 %collective-permute-start.12 = (bf16[1024,256]{1,0:T(8,128)(2,1)S(1)}, bf16[1024,256]{1,0:T(8,128)(2,1)}, u32[]{:S(2)}, u32[]{:S(2)}) collective-permute-start(bf16[1024,256]{1,0:T(8,128)(2,1)S(1)} %collective-permute-done.9.refs_10_.refs_15_), channel_id=1, source_target_pairs={{0,8},{4,12},{8,0},{12,4},{16,24},{20,28},{24,16},{28,20},{1,9},{5... | collective-permute-start | bytes 1572872 | tf_op jit(solution)/shard_map/ppermute | solution.py:616
  35.7 0.8 copy-start.11
  36.5 15.0 %collective-permute-start.1 = (bf16[1024,256]{1,0:T(8,128)(2,1)}, bf16[1024,256]{1,0:T(8,128)(2,1)}, u32[]{:S(2)}, u32[]{:S(2)}) collective-permute-start(bf16[1024,256]{1,0:T(8,128)(2,1)} %collective-permute-done.refs_2_.refs_10_), channel_id=1, source_target_pairs={{0,16},{4,20},{8,24},{12,28},{16,0},{20,4},{24,8},{28,12},{1,17},{... | collective-permute-start | bytes 1572872 | tf_op jit(solution)/shard_map/ppermute | solution.py:616
  38.0 4.6 %copy-start.1 = (bf16[768,8192]{1,0:T(8,128)(2,1)S(1)}, bf16[768,8192]{1,0:T(8,128)(2,1)}, u32[]{:S(2)}) copy-start(bf16[768,8192]{1,0:T(8,128)(2,1)} %copy-done) | copy-start | bytes 37748740
  42.6 1.0 copy-start.6
  43.7 1.0 copy-start.9
  44.7 1.0 copy-start.12
  51.4 6.7 %copy-start.3 = (bf16[768,1024]{1,0:T(8,128)(2,1)S(1)}, bf16[768,1024]{1,0:T(8,128)(2,1)}, u32[]{:S(2)}) copy-start(bf16[768,1024]{1,0:T(8,128)(2,1)} %q_ref.5) | copy-start | bytes 4718596
  51.4 2.2 %collective-permute-start.13 = (bf16[1024,256]{1,0:T(8,128)(2,1)}, bf16[1024,256]{1,0:T(8,128)(2,1)S(1)}, u32[]{:S(2)}, u32[]{:S(2)}) collective-permute-start(bf16[1024,256]{1,0:T(8,128)(2,1)} %collective-permute-done.12.refs_2_.refs_1_), channel_id=1, source_target_pairs={{0,4},{4,0},{8,12},{12,8},{16,20},{20,16},{24,28},{28,24},{1,5},{5... | collective-permute-start | bytes 1572872 | tf_op jit(solution)/shard_map/ppermute | solution.py:616
  51.5 2.8 %collective-permute-start.11 = (bf16[1024,256]{1,0:T(8,128)(2,1)}, bf16[1024,256]{1,0:T(8,128)(2,1)S(1)}, u32[]{:S(2)}, u32[]{:S(2)}) collective-permute-start(bf16[1024,256]{1,0:T(8,128)(2,1)} %collective-permute-done.1.refs_0_), channel_id=1, source_target_pairs={{0,4},{4,0},{8,12},{12,8},{16,20},{20,16},{24,28},{28,24},{1,5},{5... | collective-permute-start | bytes 1572872 | tf_op jit(solution)/shard_map/ppermute | solution.py:616
  54.3 17.0 %slice-start = ((s8[12582912]{0:T(1024)(128)(4,1)}), s8[4194304]{0:T(1024)(128)(4,1)S(1)}, s32[]{:S(2)}) async-start(s8[12582912]{0:T(1024)(128)(4,1)} %bitcast.10), calls=%async_computation | async-start | bytes 8388608
  54.3 17.0 %slice-start.1 = ((s8[12582912]{0:T(1024)(128)(4,1)}), s8[4194304]{0:T(1024)(128)(4,1)S(1)}, s32[]{:S(2)}) async-start(s8[12582912]{0:T(1024)(128)(4,1)} %bitcast.10), calls=%async_computation.1 | async-start | bytes 8388608
  58.1 6.6 %copy-start.4 = (f32[2,384,128]{2,1,0:T(8,128)S(1)}, f32[2,384,128]{2,1,0:T(8,128)}, u32[]{:S(2)}) copy-start(f32[2,384,128]{2,1,0:T(8,128)} %constant.8.clone.table_hbm.refs_5_.table_ref) | copy-start | bytes 1179652
  58.1 13.3 %slice-start.2 = ((s8[12582912]{0:T(1024)(128)(4,1)}), s8[4194304]{0:T(1024)(128)(4,1)S(1)}, s32[]{:S(2)}) async-start(s8[12582912]{0:T(1024)(128)(4,1)} %bitcast.10), calls=%async_computation.2 | async-start | bytes 8388608
  63.1 8.2 %collective-permute-start.14 = (f32[8,128]{1,0:T(8,128)S(1)}, f32[8,128]{1,0:T(8,128)S(1)}, u32[]{:S(2)}, u32[]{:S(2)}) collective-permute-start(f32[8,128]{1,0:T(8,128)S(1)} %get-tuple-element.64), channel_id=1, source_target_pairs={{0,1},{1,0},{2,3},{3,2},{4,5},{5,4},{6,7},{7,6},{8,9},{9,8},{10,11... | collective-permute-start | bytes 12296 | tf_op jit(solution)/shard_map/ppermute | solution.py:616
  72.4 9.5 %collective-permute-start.17 = (bf16[2,256,1024]{2,1,0:T(8,128)(2,1)S(1)}, bf16[2,256,1024]{2,1,0:T(8,128)(2,1)S(1)}, u32[]{:S(2)}, u32[]{:S(2)}) collective-permute-start(bf16[2,256,1024]{2,1,0:T(8,128)(2,1)S(1)} %gradient_block.2), channel_id=1, source_target_pairs={{0,4},{4,0},{8,12},{12,8},{16,20},{20,16},{24,28},{28,24},{1,5},{5... | collective-permute-start | bytes 3145736 | tf_op jit(solution)/shard_map/ppermute | solution.py:616
  75.2 9.4 %collective-permute-start.18 = (bf16[2,256,1024]{2,1,0:T(8,128)(2,1)S(1)}, bf16[2,256,1024]{2,1,0:T(8,128)(2,1)S(1)}, u32[]{:S(2)}, u32[]{:S(2)}) collective-permute-start(bf16[2,256,1024]{2,1,0:T(8,128)(2,1)S(1)} %get-tuple-element.69), channel_id=1, source_target_pairs={{0,4},{4,0},{8,12},{12,8},{16,20},{20,16},{24,28},{28,24},{1,5},{5... | collective-permute-start | bytes 3145736 | tf_op jit(solution)/shard_map/ppermute | solution.py:616
  75.7 8.8 %collective-permute-start.19 = (bf16[2,256,1024]{2,1,0:T(8,128)(2,1)S(1)}, bf16[2,256,1024]{2,1,0:T(8,128)(2,1)S(1)}, u32[]{:S(2)}, u32[]{:S(2)}) collective-permute-start(bf16[2,256,1024]{2,1,0:T(8,128)(2,1)S(1)} %get-tuple-element.70), channel_id=1, source_target_pairs={{0,4},{4,0},{8,12},{12,8},{16,20},{20,16},{24,28},{28,24},{1,5},{5... | collective-permute-start | bytes 3145736 | tf_op jit(solution)/shard_map/ppermute | solution.py:616
  75.8 8.8 %collective-permute-start.20 = (bf16[2,256,1024]{2,1,0:T(8,128)(2,1)S(1)}, bf16[2,256,1024]{2,1,0:T(8,128)(2,1)S(1)}, u32[]{:S(2)}, u32[]{:S(2)}) collective-permute-start(bf16[2,256,1024]{2,1,0:T(8,128)(2,1)S(1)} %get-tuple-element.71), channel_id=1, source_target_pairs={{0,4},{4,0},{8,12},{12,8},{16,20},{20,16},{24,28},{28,24},{1,5},{5... | collective-permute-start | bytes 3145736 | tf_op jit(solution)/shard_map/ppermute | solution.py:616
  76.2 4.5 %collective-permute-start.15 = (f32[8,128]{1,0:T(8,128)S(1)}, f32[8,128]{1,0:T(8,128)S(1)}, u32[]{:S(2)}, u32[]{:S(2)}) collective-permute-start(f32[8,128]{1,0:T(8,128)S(1)} %add.27), channel_id=1, source_target_pairs={{0,2},{1,3},{2,0},{3,1},{4,6},{5,7},{6,4},{7,5},{8,10},{9,11},{10,... | collective-permute-start | bytes 12296 | tf_op jit(solution)/shard_map/ppermute | solution.py:616
  80.7 1.2 collective-permute-start.16
  83.0 14.8 %collective-permute-start.25 = (bf16[256,1024]{1,0:T(8,128)(2,1)S(1)}, bf16[256,1024]{1,0:T(8,128)(2,1)S(1)}, u32[]{:S(2)}, u32[]{:S(2)}) collective-permute-start(bf16[256,1024]{1,0:T(8,128)(2,1)S(1)} %get-tuple-element.75), channel_id=1, source_target_pairs={{0,8},{4,12},{8,0},{12,4},{16,24},{20,28},{24,16},{28,20},{1,9},{5... | collective-permute-start | bytes 1572872 | tf_op jit(solution)/shard_map/ppermute | solution.py:616
  83.6 15.0 %collective-permute-start.22 = (bf16[256,1024]{1,0:T(8,128)(2,1)S(1)}, bf16[256,1024]{1,0:T(8,128)(2,1)S(1)}, u32[]{:S(2)}, u32[]{:S(2)}) collective-permute-start(bf16[256,1024]{1,0:T(8,128)(2,1)S(1)} %get-tuple-element.74), channel_id=1, source_target_pairs={{0,16},{4,20},{8,24},{12,28},{16,0},{20,4},{24,8},{28,12},{1,17},{... | collective-permute-start | bytes 1572872 | tf_op jit(solution)/shard_map/ppermute | solution.py:616
  87.9 21.8 %collective-permute-start.21 = (bf16[256,1024]{1,0:T(8,128)(2,1)S(1)}, bf16[256,1024]{1,0:T(8,128)(2,1)S(1)}, u32[]{:S(2)}, u32[]{:S(2)}) collective-permute-start(bf16[256,1024]{1,0:T(8,128)(2,1)S(1)} %get-tuple-element.78), channel_id=1, source_target_pairs={{0,16},{4,20},{8,24},{12,28},{16,0},{20,4},{24,8},{28,12},{1,17},{... | collective-permute-start | bytes 1572872 | tf_op jit(solution)/shard_map/ppermute | solution.py:616
  89.0 20.6 %collective-permute-start.24 = (bf16[256,1024]{1,0:T(8,128)(2,1)S(1)}, bf16[256,1024]{1,0:T(8,128)(2,1)S(1)}, u32[]{:S(2)}, u32[]{:S(2)}) collective-permute-start(bf16[256,1024]{1,0:T(8,128)(2,1)S(1)} %get-tuple-element.81), channel_id=1, source_target_pairs={{0,8},{4,12},{8,0},{12,4},{16,24},{20,28},{24,16},{28,20},{1,9},{5... | collective-permute-start | bytes 1572872 | tf_op jit(solution)/shard_map/ppermute | solution.py:616
  98.0 21.7 %collective-permute-start.26 = (bf16[256,1024]{1,0:T(8,128)(2,1)S(1)}, bf16[256,1024]{1,0:T(8,128)(2,1)S(1)}, u32[]{:S(2)}, u32[]{:S(2)}) collective-permute-start(bf16[256,1024]{1,0:T(8,128)(2,1)S(1)} %add_convert_fusion), channel_id=1, source_target_pairs={{0,16},{4,20},{8,24},{12,28},{16,0},{20,4},{24,8},{28,12},{1,17},{... | collective-permute-start | bytes 1572872 | tf_op jit(solution)/shard_map/ppermute | solution.py:616
  98.8 21.0 %collective-permute-start.23 = (bf16[256,1024]{1,0:T(8,128)(2,1)S(1)}, bf16[256,1024]{1,0:T(8,128)(2,1)S(1)}, u32[]{:S(2)}, u32[]{:S(2)}) collective-permute-start(bf16[256,1024]{1,0:T(8,128)(2,1)S(1)} %add_convert_fusion.1), channel_id=1, source_target_pairs={{0,8},{4,12},{8,0},{12,4},{16,24},{20,28},{24,16},{28,20},{1,9},{5... | collective-permute-start | bytes 1572872 | tf_op jit(solution)/shard_map/ppermute | solution.py:616
  120.5 28.5 %collective-permute-start.35 = (bf16[2,1024,256]{2,1,0:T(8,128)(2,1)S(1)}, bf16[2,1024,256]{2,1,0:T(8,128)(2,1)S(1)}, u32[]{:S(2)}, u32[]{:S(2)}) collective-permute-start(bf16[2,1024,256]{2,1,0:T(8,128)(2,1)S(1)} %get-tuple-element.86.refs_0_), channel_id=1, source_target_pairs={{0,16},{4,20},{8,24},{12,28},{16,0},{20,4},{24,8},{28,12},{1,17},{... | collective-permute-start | bytes 3145736 | tf_op jit(solution)/shard_map/ppermute | solution.py:616
  121.5 28.7 %collective-permute-start.33 = (bf16[2,1024,256]{2,1,0:T(8,128)(2,1)S(1)}, bf16[2,1024,256]{2,1,0:T(8,128)(2,1)S(1)}, u32[]{:S(2)}, u32[]{:S(2)}) collective-permute-start(bf16[2,1024,256]{2,1,0:T(8,128)(2,1)S(1)} %get-tuple-element.86.refs_0_), channel_id=1, source_target_pairs={{0,8},{4,12},{8,0},{12,4},{16,24},{20,28},{24,16},{28,20},{1,9},{5... | collective-permute-start | bytes 3145736 | tf_op jit(solution)/shard_map/ppermute | solution.py:616
  122.5 3.6 %collective-permute-start.27 = (f32[8,128]{1,0:T(8,128)S(1)}, f32[8,128]{1,0:T(8,128)S(1)}, u32[]{:S(2)}, u32[]{:S(2)}) collective-permute-start(f32[8,128]{1,0:T(8,128)S(1)} %get-tuple-element.85), channel_id=1, source_target_pairs={{0,1},{1,0},{2,3},{3,2},{4,5},{5,4},{6,7},{7,6},{8,9},{9,8},{10,11... | collective-permute-start | bytes 12296 | tf_op jit(solution)/shard_map/ppermute | solution.py:616
  126.1 4.5 %collective-permute-start.28 = (f32[8,128]{1,0:T(8,128)S(1)}, f32[8,128]{1,0:T(8,128)S(1)}, u32[]{:S(2)}, u32[]{:S(2)}) collective-permute-start(f32[8,128]{1,0:T(8,128)S(1)} %add.31), channel_id=1, source_target_pairs={{0,2},{1,3},{2,0},{3,1},{4,6},{5,7},{6,4},{7,5},{8,10},{9,11},{10,... | collective-permute-start | bytes 12296 | tf_op jit(solution)/shard_map/ppermute | solution.py:616
  130.7 1.2 collective-permute-start.29
  131.8 13.5 %collective-permute-start.30 = (f32[8,128]{1,0:T(8,128)S(1)}, f32[8,128]{1,0:T(8,128)S(1)}, u32[]{:S(2)}, u32[]{:S(2)}) collective-permute-start(f32[8,128]{1,0:T(8,128)S(1)} %add.33), channel_id=1, source_target_pairs={{0,8},{4,12},{8,0},{12,4},{16,24},{20,28},{24,16},{28,20},{1,9},{5... | collective-permute-start | bytes 12296 | tf_op jit(solution)/shard_map/ppermute | solution.py:616
  145.3 3.6 %collective-permute-start.31 = (f32[8,128]{1,0:T(8,128)S(1)}, f32[8,128]{1,0:T(8,128)S(1)}, u32[]{:S(2)}, u32[]{:S(2)}) collective-permute-start(f32[8,128]{1,0:T(8,128)S(1)} %add.34), channel_id=1, source_target_pairs={{0,16},{4,20},{8,24},{12,28},{16,0},{20,4},{24,8},{28,12},{1,17},{... | collective-permute-start | bytes 12296 | tf_op jit(solution)/shard_map/ppermute | solution.py:616
  146.5 18.7 %collective-permute-start.32 = (bf16[2,1024,256]{2,1,0:T(8,128)(2,1)S(1)}, bf16[2,1024,256]{2,1,0:T(8,128)(2,1)S(1)}, u32[]{:S(2)}, u32[]{:S(2)}) collective-permute-start(bf16[2,1024,256]{2,1,0:T(8,128)(2,1)S(1)} %get-tuple-element.86.refs_0_), channel_id=1, source_target_pairs={{0,4},{4,0},{8,12},{12,8},{16,20},{20,16},{24,28},{28,24},{1,5},{5... | collective-permute-start | bytes 3145736 | tf_op jit(solution)/shard_map/ppermute | solution.py:616
  149.0 12.0 %collective-permute-start.39 = (bf16[1024,256]{1,0:T(8,128)(2,1)S(1)}, bf16[1024,256]{1,0:T(8,128)(2,1)S(1)}, u32[]{:S(2)}, u32[]{:S(2)}) collective-permute-start(bf16[1024,256]{1,0:T(8,128)(2,1)S(1)} %slice_bitcast_fusion), channel_id=1, source_target_pairs={{0,8},{4,12},{8,0},{12,4},{16,24},{20,28},{24,16},{28,20},{1,9},{5... | collective-permute-start | bytes 1572872 | tf_op jit(solution)/shard_map/ppermute | solution.py:616
  150.2 15.0 %copy-start.7 = (bf16[1024,256]{1,0:T(8,128)(2,1)S(1)}, bf16[1024,256]{1,0:T(8,128)(2,1)}, u32[]{:S(2)}) copy-start(bf16[1024,256]{1,0:T(8,128)(2,1)} %copy-done.5) | copy-start | bytes 1572868
  150.2 15.0 %copy-start.10 = (bf16[1024,256]{1,0:T(8,128)(2,1)S(1)}, bf16[1024,256]{1,0:T(8,128)(2,1)}, u32[]{:S(2)}) copy-start(bf16[1024,256]{1,0:T(8,128)(2,1)} %copy-done.8) | copy-start | bytes 1572868
  150.2 15.0 %copy-start.13 = (bf16[1024,256]{1,0:T(8,128)(2,1)S(1)}, bf16[1024,256]{1,0:T(8,128)(2,1)}, u32[]{:S(2)}) copy-start(bf16[1024,256]{1,0:T(8,128)(2,1)} %copy-done.11) | copy-start | bytes 1572868
  150.2 15.0 %collective-permute-start.34 = (bf16[2,1024,256]{2,1,0:T(8,128)(2,1)S(1)}, bf16[2,1024,256]{2,1,0:T(8,128)(2,1)S(1)}, u32[]{:S(2)}, u32[]{:S(2)}) collective-permute-start(bf16[2,1024,256]{2,1,0:T(8,128)(2,1)S(1)} %collective-permute-done.33.refs_2_), channel_id=1, source_target_pairs={{0,4},{4,0},{8,12},{12,8},{16,20},{20,16},{24,28},{28,24},{1,5},{5... | collective-permute-start | bytes 3145736 | tf_op jit(solution)/shard_map/ppermute | solution.py:616
  150.3 14.9 %collective-permute-start.36 = (bf16[2,1024,256]{2,1,0:T(8,128)(2,1)S(1)}, bf16[2,1024,256]{2,1,0:T(8,128)(2,1)S(1)}, u32[]{:S(2)}, u32[]{:S(2)}) collective-permute-start(bf16[2,1024,256]{2,1,0:T(8,128)(2,1)S(1)} %collective-permute-done.35.refs_4_), channel_id=1, source_target_pairs={{0,4},{4,0},{8,12},{12,8},{16,20},{20,16},{24,28},{28,24},{1,5},{5... | collective-permute-start | bytes 3145736 | tf_op jit(solution)/shard_map/ppermute | solution.py:616
  150.8 13.9 %collective-permute-start.37 = (bf16[1024,256]{1,0:T(8,128)(2,1)S(1)}, bf16[1024,256]{1,0:T(8,128)(2,1)S(1)}, u32[]{:S(2)}, u32[]{:S(2)}) collective-permute-start(bf16[1024,256]{1,0:T(8,128)(2,1)S(1)} %slice_bitcast_fusion.1), channel_id=1, source_target_pairs={{0,16},{4,20},{8,24},{12,28},{16,0},{20,4},{24,8},{28,12},{1,17},{... | collective-permute-start | bytes 1572872 | tf_op jit(solution)/shard_map/ppermute | solution.py:616
  161.0 14.9 %collective-permute-start.40 = (bf16[1024,256]{1,0:T(8,128)(2,1)S(1)}, bf16[1024,256]{1,0:T(8,128)(2,1)S(1)}, u32[]{:S(2)}, u32[]{:S(2)}) collective-permute-start(bf16[1024,256]{1,0:T(8,128)(2,1)S(1)} %collective-permute-done.39.refs_1_), channel_id=1, source_target_pairs={{0,4},{4,0},{8,12},{12,8},{16,20},{20,16},{24,28},{28,24},{1,5},{5... | collective-permute-start | bytes 1572872 | tf_op jit(solution)/shard_map/ppermute | solution.py:616
  164.7 11.2 %collective-permute-start.38 = (bf16[1024,256]{1,0:T(8,128)(2,1)S(1)}, bf16[1024,256]{1,0:T(8,128)(2,1)S(1)}, u32[]{:S(2)}, u32[]{:S(2)}) collective-permute-start(bf16[1024,256]{1,0:T(8,128)(2,1)S(1)} %collective-permute-done.37.refs_0_), channel_id=1, source_target_pairs={{0,4},{4,0},{8,12},{12,8},{16,20},{20,16},{24,28},{28,24},{1,5},{5... | collective-permute-start | bytes 1572872 | tf_op jit(solution)/shard_map/ppermute | solution.py:616
